TPU v7x, 32 devices: a whole 2x2x4 slice. The times are simulated.
32 devices in a mesh: member: 16 (over z, y, x), row: 2 (over core).
Axes of the slice: x: 2, y: 2, z: 4, core: 2. Of those that a mesh axis runs over, the one named last changes fastest.
Arguments:
- fields: float32 [32, 3, 32, 1024], P('member', None, 'row'), may hold values from -1.5 to 1.5
- bathymetry: int32 [32, 1024], P('row'), may hold values from 250 to 300
- copy_lists: int32 [3, 5, 32], replicated, may hold values from 0 to 31, as said below
Outputs:
- final_fields: float32 [32, 3, 32, 1024], P('member', None, 'row')
Inputs may be any that keep to these rules, and one draw needn't show every extreme that they name: copy_lists[c, s, m] is m or m xor 2 to the power s; members m and m xor 2 to the power s either both keep their own state or both take the same one of the two.
All inputs are finite; a program needn't handle non-finite values.
Results may differ from a plain program's by a relative error of at most 0.00002.
Values sent between devices are 32-bit elements; how exact they have to be, the bound alone decides.
A program may use at most 64 MiB of HBM per device.

v0:
```python
import jax
import jax.numpy as jnp
from jax import lax
from jax.sharding import PartitionSpec as P

STEPS = 4
CYCLES = 3


gravity = 2.0
coriolis = 0.1
friction = 0.02
time_step = 0.25


def extended(x, sides, width):
    for axis, dim in sides:
        devices, length = (lax.axis_size(axis), x.shape[dim])
        up = [(i, (i + 1) % devices) for i in range(devices)]
        down = [(j, i) for i, j in up]
        last = lax.slice_in_dim(x, length - width, length, axis=dim)
        leading = lax.slice_in_dim(x, 0, width, axis=dim)
        before = lax.ppermute(last, axis, up)
        after = lax.ppermute(leading, axis, down)
        x = jnp.concatenate([before, x, after], axis=dim)
    return x


def partner(block, axis, bit):
    count = lax.axis_size(axis)
    route = []
    for low in range(count):
        high = low | 1 << bit
        if high != low and high < count:
            route += [(low, high), (high, low)]
    return lax.ppermute(block, axis, route)


def rates(padded, depth_pad):
    height = padded[:, 0]
    east = padded[:, 1]
    north = padded[:, 2]
    column = depth_pad + height
    flux_x = column * east
    flux_y = column * north
    diff_x = (jnp.roll(flux_x, -1, -1) - jnp.roll(flux_x, 1, -1))[:, 1:-1]
    diff_y = flux_y[:, 2:] - flux_y[:, :-2]
    rate_h = -0.5 * (diff_x + diff_y)
    slope_x = (jnp.roll(height, -1, -1) - jnp.roll(height, 1, -1))[:, 1:-1]
    slope_y = height[:, 2:] - height[:, :-2]
    east_mid = east[:, 1:-1]
    north_mid = north[:, 1:-1]
    rate_u = -0.5 * gravity * slope_x + coriolis * north_mid - friction * east_mid
    rate_v = -0.5 * gravity * slope_y - coriolis * east_mid - friction * north_mid
    return jnp.stack([rate_h, rate_u, rate_v], 1)


def trim_depth(depth_full, width):
    offset = 2 * STEPS - width
    total = depth_full.shape[0]
    return depth_full[offset : total - offset]


def body(fields, bathymetry, copy_lists):
    depth_ext = extended(bathymetry, (("row", 0),), 2 * STEPS)
    depth_full = depth_ext.astype(jnp.float32) / 100.0
    local_count = fields.shape[0]
    section_count = copy_lists.shape[1]
    member_index = lax.axis_index("member")
    own_members = local_count * member_index + jnp.arange(local_count, dtype=jnp.int32)
    current = fields
    for cycle_no in range(CYCLES):
        padded = extended(current, (("row", 2),), 2 * STEPS)
        for step_no in range(STEPS):
            width = 2 * (STEPS - step_no)
            first_rate = rates(padded, trim_depth(depth_full, width))
            rows_now = padded.shape[2]
            middle = padded[:, :, 1 : rows_now - 1] + time_step * first_rate
            second_rate = rates(middle, trim_depth(depth_full, width - 1))
            rows_mid = first_rate.shape[2]
            padded = padded[:, :, 2 : rows_now - 2] + 0.5 * time_step * (
                first_rate[:, :, 1 : rows_mid - 1] + second_rate
            )
        current = padded
        lists_now = copy_lists[cycle_no]
        sources = lax.dynamic_slice_in_dim(lists_now[0], local_count * member_index, local_count)
        current = jnp.take(current, sources - local_count * member_index, axis=0)
        for section_no in range(1, section_count):
            sources = lax.dynamic_slice_in_dim(
                lists_now[section_no], local_count * member_index, local_count
            )
            arrived = partner(current, "member", section_no - 1)
            taken = (sources != own_members)[:, None, None, None]
            current = jnp.where(taken, arrived, current)
    return current


def solution(mesh):
    placed = (P("member", None, "row", None), P("row", None), P())
    return jax.shard_map(
        body, mesh=mesh, in_specs=placed, out_specs=P("member", None, "row", None), check_vma=False
    )
```

profile of v0, /device:TPU:0, one launch (start us, length us, event | category | flops | bytes accessed | tf_op | source)
XLA Modules:
  0.0 189.3 jit_solution(792022510514850254)
XLA Ops:
  0.0 0.8 fusion.462
  1.3 1.0 fusion.365
  3.1 0.6 copy-done.2
  4.0 0.9 copy-done
  13.4 0.6 gather_fusion
  14.0 2.6 %collective-permute-start.4 = (f32[2,3,16,1024]{3,2,1,0:T(8,128)S(1)}, f32[2,3,16,1024]{3,2,1,0:T(8,128)S(1)}, u32[]{:S(2)}, u32[]{:S(2)}) collective-permute-start(f32[2,3,16,1024]{3,2,1,0:T(8,128)S(1)} %broadcast_select_fusion.2), channel_id=1, source_target_pairs={{0,2},{2,0},{4,6},{6,4},{8,10},{10,8},{12,14},{14,12},{16,18},{18,... | collective-permute-start | bytes 1179656 | tf_op jit(solution)/shard_map/ppermute | solution.py:36
  16.7 9.6 %collective-permute-done.4 = f32[2,3,16,1024]{3,2,1,0:T(8,128)S(1)} collective-permute-done((f32[2,3,16,1024]{3,2,1,0:T(8,128)S(1)}, f32[2,3,16,1024]{3,2,1,0:T(8,128)S(1)}, u32[]{:S(2)}, u32[]{:S(2)}) %collective-permute-start.4) | collective-permute-done | bytes 393248 | tf_op jit(solution)/shard_map/ppermute | solution.py:36
  26.5 1.8 collective-permute-start.5
  28.4 9.0 %collective-permute-done.5 = f32[2,3,16,1024]{3,2,1,0:T(8,128)S(1)} collective-permute-done((f32[2,3,16,1024]{3,2,1,0:T(8,128)S(1)}, f32[2,3,16,1024]{3,2,1,0:T(8,128)S(1)}, u32[]{:S(2)}, u32[]{:S(2)}) %collective-permute-start.5) | collective-permute-done | bytes 393248 | tf_op jit(solution)/shard_map/ppermute | solution.py:36
  37.6 1.7 collective-permute-start.6
  39.3 8.3 %collective-permute-done.6 = f32[2,3,16,1024]{3,2,1,0:T(8,128)S(1)} collective-permute-done((f32[2,3,16,1024]{3,2,1,0:T(8,128)S(1)}, f32[2,3,16,1024]{3,2,1,0:T(8,128)S(1)}, u32[]{:S(2)}, u32[]{:S(2)}) %collective-permute-start.6) | collective-permute-done | bytes 393248 | tf_op jit(solution)/shard_map/ppermute | solution.py:36
  47.8 2.4 %collective-permute-start.7 = (f32[2,3,16,1024]{3,2,1,0:T(8,128)S(1)}, f32[2,3,16,1024]{3,2,1,0:T(8,128)S(1)}, u32[]{:S(2)}, u32[]{:S(2)}) collective-permute-start(f32[2,3,16,1024]{3,2,1,0:T(8,128)S(1)} %broadcast_select_fusion.5), channel_id=1, source_target_pairs={{0,16},{16,0},{2,18},{18,2},{4,20},{20,4},{6,22},{22,6},{8,24},{24... | collective-permute-start | bytes 1179656 | tf_op jit(solution)/shard_map/ppermute | solution.py:36
  50.3 16.0 %collective-permute-done.7 = f32[2,3,16,1024]{3,2,1,0:T(8,128)S(1)} collective-permute-done((f32[2,3,16,1024]{3,2,1,0:T(8,128)S(1)}, f32[2,3,16,1024]{3,2,1,0:T(8,128)S(1)}, u32[]{:S(2)}, u32[]{:S(2)}) %collective-permute-start.7) | collective-permute-done | bytes 393248 | tf_op jit(solution)/shard_map/ppermute | solution.py:36
  67.0 0.9 collective-permute-done.8
  77.0 0.6 gather_fusion.1
  77.7 1.1 collective-permute-start.10
  78.9 10.1 %collective-permute-done.10 = f32[2,3,16,1024]{3,2,1,0:T(8,128)S(1)} collective-permute-done((f32[2,3,16,1024]{3,2,1,0:T(8,128)S(1)}, f32[2,3,16,1024]{3,2,1,0:T(8,128)S(1)}, u32[]{:S(2)}, u32[]{:S(2)}) %collective-permute-start.10) | collective-permute-done | bytes 393248 | tf_op jit(solution)/shard_map/ppermute | solution.py:36
  89.1 1.1 collective-permute-start.11
  90.3 9.3 %collective-permute-done.11 = f32[2,3,16,1024]{3,2,1,0:T(8,128)S(1)} collective-permute-done((f32[2,3,16,1024]{3,2,1,0:T(8,128)S(1)}, f32[2,3,16,1024]{3,2,1,0:T(8,128)S(1)}, u32[]{:S(2)}, u32[]{:S(2)}) %collective-permute-start.11) | collective-permute-done | bytes 393248 | tf_op jit(solution)/shard_map/ppermute | solution.py:36
  100.1 9.2 %collective-permute-done.12 = f32[2,3,16,1024]{3,2,1,0:T(8,128)S(1)} collective-permute-done((f32[2,3,16,1024]{3,2,1,0:T(8,128)S(1)}, f32[2,3,16,1024]{3,2,1,0:T(8,128)S(1)}, u32[]{:S(2)}, u32[]{:S(2)}) %collective-permute-start.12) | collective-permute-done | bytes 393248 | tf_op jit(solution)/shard_map/ppermute | solution.py:36
  109.5 1.9 %collective-permute-start.13 = (f32[2,3,16,1024]{3,2,1,0:T(8,128)S(1)}, f32[2,3,16,1024]{3,2,1,0:T(8,128)S(1)}, u32[]{:S(2)}, u32[]{:S(2)}) collective-permute-start(f32[2,3,16,1024]{3,2,1,0:T(8,128)S(1)} %broadcast_select_fusion.9), channel_id=1, source_target_pairs={{0,16},{16,0},{2,18},{18,2},{4,20},{20,4},{6,22},{22,6},{8,24},{24... | collective-permute-start | bytes 1179656 | tf_op jit(solution)/shard_map/ppermute | solution.py:36
  111.5 16.0 %collective-permute-done.13 = f32[2,3,16,1024]{3,2,1,0:T(8,128)S(1)} collective-permute-done((f32[2,3,16,1024]{3,2,1,0:T(8,128)S(1)}, f32[2,3,16,1024]{3,2,1,0:T(8,128)S(1)}, u32[]{:S(2)}, u32[]{:S(2)}) %collective-permute-start.13) | collective-permute-done | bytes 393248 | tf_op jit(solution)/shard_map/ppermute | solution.py:36
  128.2 0.9 collective-permute-done.14
  138.0 0.6 gather_fusion.2
  138.7 1.1 collective-permute-start.16
  139.9 10.1 %collective-permute-done.16 = f32[2,3,16,1024]{3,2,1,0:T(8,128)S(1)} collective-permute-done((f32[2,3,16,1024]{3,2,1,0:T(8,128)S(1)}, f32[2,3,16,1024]{3,2,1,0:T(8,128)S(1)}, u32[]{:S(2)}, u32[]{:S(2)}) %collective-permute-start.16) | collective-permute-done | bytes 393248 | tf_op jit(solution)/shard_map/ppermute | solution.py:36
  150.2 1.1 collective-permute-start.17
  151.4 9.3 %collective-permute-done.17 = f32[2,3,16,1024]{3,2,1,0:T(8,128)S(1)} collective-permute-done((f32[2,3,16,1024]{3,2,1,0:T(8,128)S(1)}, f32[2,3,16,1024]{3,2,1,0:T(8,128)S(1)}, u32[]{:S(2)}, u32[]{:S(2)}) %collective-permute-start.17) | collective-permute-done | bytes 393248 | tf_op jit(solution)/shard_map/ppermute | solution.py:36
  161.1 9.2 %collective-permute-done.18 = f32[2,3,16,1024]{3,2,1,0:T(8,128)S(1)} collective-permute-done((f32[2,3,16,1024]{3,2,1,0:T(8,128)S(1)}, f32[2,3,16,1024]{3,2,1,0:T(8,128)S(1)}, u32[]{:S(2)}, u32[]{:S(2)}) %collective-permute-start.18) | collective-permute-done | bytes 393248 | tf_op jit(solution)/shard_map/ppermute | solution.py:36
  170.5 1.9 %collective-permute-start.19 = (f32[2,3,16,1024]{3,2,1,0:T(8,128)S(1)}, f32[2,3,16,1024]{3,2,1,0:T(8,128)S(1)}, u32[]{:S(2)}, u32[]{:S(2)}) collective-permute-start(f32[2,3,16,1024]{3,2,1,0:T(8,128)S(1)} %broadcast_select_fusion.13), channel_id=1, source_target_pairs={{0,16},{16,0},{2,18},{18,2},{4,20},{20,4},{6,22},{22,6},{8,24},{24... | collective-permute-start | bytes 1179656 | tf_op jit(solution)/shard_map/ppermute | solution.py:36
  172.4 16.0 %collective-permute-done.19 = f32[2,3,16,1024]{3,2,1,0:T(8,128)S(1)} collective-permute-done((f32[2,3,16,1024]{3,2,1,0:T(8,128)S(1)}, f32[2,3,16,1024]{3,2,1,0:T(8,128)S(1)}, u32[]{:S(2)}, u32[]{:S(2)}) %collective-permute-start.19) | collective-permute-done | bytes 393248 | tf_op jit(solution)/shard_map/ppermute | solution.py:36
  188.4 0.9 broadcast_select_fusion.14
  (285 shorter events, 30.8 us)
Async XLA Ops:
  0.8 3.0 %collective-permute-start.2 = (s32[8,1024]{1,0:T(8,128)S(1)}, s32[8,1024]{1,0:T(8,128)S(1)}, u32[]{:S(2)}, u32[]{:S(2)}) collective-permute-start(s32[8,1024]{1,0:T(8,128)S(1)} %get-tuple-element.402), channel_id=1, source_target_pairs={{0,1},{1,0},{2,3},{3,2},{4,5},{5,4},{6,7},{7,6},{8,9},{9,8},{10,11... | collective-permute-start | bytes 98312 | tf_op jit(solution)/shard_map/ppermute | solution.py:23
  1.2 2.5 %collective-permute-start.3 = (s32[8,1024]{1,0:T(8,128)S(1)}, s32[8,1024]{1,0:T(8,128)S(1)}, u32[]{:S(2)}, u32[]{:S(2)}) collective-permute-start(s32[8,1024]{1,0:T(8,128)S(1)} %get-tuple-element.403), channel_id=1, source_target_pairs={{1,0},{0,1},{3,2},{2,3},{5,4},{4,5},{7,6},{6,7},{9,8},{8,9},{11,10... | collective-permute-start | bytes 98312 | tf_op jit(solution)/shard_map/ppermute | solution.py:24
  2.4 1.6 collective-permute-start
  2.9 0.9 copy-start.1
  2.9 0.7 copy-start.2
  2.9 2.0 %collective-permute-start.1 = (f32[2,3,8,1024]{3,2,0,1:T(8,128)S(1)}, f32[2,3,8,1024]{3,2,0,1:T(8,128)S(1)}, u32[]{:S(2)}, u32[]{:S(2)}) collective-permute-start(f32[2,3,8,1024]{3,2,0,1:T(8,128)S(1)} %copy.73), channel_id=1, source_target_pairs={{1,0},{0,1},{3,2},{2,3},{5,4},{4,5},{7,6},{6,7},{9,8},{8,9},{11,10... | collective-permute-start | bytes 589832 | tf_op jit(solution)/shard_map/ppermute | solution.py:24
  3.9 1.0 copy-start
  14.0 12.3 %collective-permute-start.4 = (f32[2,3,16,1024]{3,2,1,0:T(8,128)S(1)}, f32[2,3,16,1024]{3,2,1,0:T(8,128)S(1)}, u32[]{:S(2)}, u32[]{:S(2)}) collective-permute-start(f32[2,3,16,1024]{3,2,1,0:T(8,128)S(1)} %broadcast_select_fusion.2), channel_id=1, source_target_pairs={{0,2},{2,0},{4,6},{6,4},{8,10},{10,8},{12,14},{14,12},{16,18},{18,... | collective-permute-start | bytes 1179656 | tf_op jit(solution)/shard_map/ppermute | solution.py:36
  26.5 10.9 %collective-permute-start.5 = (f32[2,3,16,1024]{3,2,1,0:T(8,128)S(1)}, f32[2,3,16,1024]{3,2,1,0:T(8,128)S(1)}, u32[]{:S(2)}, u32[]{:S(2)}) collective-permute-start(f32[2,3,16,1024]{3,2,1,0:T(8,128)S(1)} %broadcast_select_fusion.3), channel_id=1, source_target_pairs={{0,4},{4,0},{2,6},{6,2},{8,12},{12,8},{10,14},{14,10},{16,20},{20,... | collective-permute-start | bytes 1179656 | tf_op jit(solution)/shard_map/ppermute | solution.py:36
  37.6 10.1 %collective-permute-start.6 = (f32[2,3,16,1024]{3,2,1,0:T(8,128)S(1)}, f32[2,3,16,1024]{3,2,1,0:T(8,128)S(1)}, u32[]{:S(2)}, u32[]{:S(2)}) collective-permute-start(f32[2,3,16,1024]{3,2,1,0:T(8,128)S(1)} %broadcast_select_fusion.4), channel_id=1, source_target_pairs={{0,8},{8,0},{2,10},{10,2},{4,12},{12,4},{6,14},{14,6},{16,24},{24,... | collective-permute-start | bytes 1179656 | tf_op jit(solution)/shard_map/ppermute | solution.py:36
  47.8 18.5 %collective-permute-start.7 = (f32[2,3,16,1024]{3,2,1,0:T(8,128)S(1)}, f32[2,3,16,1024]{3,2,1,0:T(8,128)S(1)}, u32[]{:S(2)}, u32[]{:S(2)}) collective-permute-start(f32[2,3,16,1024]{3,2,1,0:T(8,128)S(1)} %broadcast_select_fusion.5), channel_id=1, source_target_pairs={{0,16},{16,0},{2,18},{18,2},{4,20},{20,4},{6,22},{22,6},{8,24},{24... | collective-permute-start | bytes 1179656 | tf_op jit(solution)/shard_map/ppermute | solution.py:36
  66.4 1.5 collective-permute-start.8
  66.5 1.7 collective-permute-start.9
  77.7 11.3 %collective-permute-start.10 = (f32[2,3,16,1024]{3,2,1,0:T(8,128)S(1)}, f32[2,3,16,1024]{3,2,1,0:T(8,128)S(1)}, u32[]{:S(2)}, u32[]{:S(2)}) collective-permute-start(f32[2,3,16,1024]{3,2,1,0:T(8,128)S(1)} %broadcast_select_fusion.1), channel_id=1, source_target_pairs={{0,2},{2,0},{4,6},{6,4},{8,10},{10,8},{12,14},{14,12},{16,18},{18,... | collective-permute-start | bytes 1179656 | tf_op jit(solution)/shard_map/ppermute | solution.py:36
  89.1 10.5 %collective-permute-start.11 = (f32[2,3,16,1024]{3,2,1,0:T(8,128)S(1)}, f32[2,3,16,1024]{3,2,1,0:T(8,128)S(1)}, u32[]{:S(2)}, u32[]{:S(2)}) collective-permute-start(f32[2,3,16,1024]{3,2,1,0:T(8,128)S(1)} %broadcast_select_fusion.7), channel_id=1, source_target_pairs={{0,4},{4,0},{2,6},{6,2},{8,12},{12,8},{10,14},{14,10},{16,20},{20,... | collective-permute-start | bytes 1179656 | tf_op jit(solution)/shard_map/ppermute | solution.py:36
  99.8 9.6 %collective-permute-start.12 = (f32[2,3,16,1024]{3,2,1,0:T(8,128)S(1)}, f32[2,3,16,1024]{3,2,1,0:T(8,128)S(1)}, u32[]{:S(2)}, u32[]{:S(2)}) collective-permute-start(f32[2,3,16,1024]{3,2,1,0:T(8,128)S(1)} %broadcast_select_fusion.8), channel_id=1, source_target_pairs={{0,8},{8,0},{2,10},{10,2},{4,12},{12,4},{6,14},{14,6},{16,24},{24,... | collective-permute-start | bytes 1179656 | tf_op jit(solution)/shard_map/ppermute | solution.py:36
  109.5 18.0 %collective-permute-start.13 = (f32[2,3,16,1024]{3,2,1,0:T(8,128)S(1)}, f32[2,3,16,1024]{3,2,1,0:T(8,128)S(1)}, u32[]{:S(2)}, u32[]{:S(2)}) collective-permute-start(f32[2,3,16,1024]{3,2,1,0:T(8,128)S(1)} %broadcast_select_fusion.9), channel_id=1, source_target_pairs={{0,16},{16,0},{2,18},{18,2},{4,20},{20,4},{6,22},{22,6},{8,24},{24... | collective-permute-start | bytes 1179656 | tf_op jit(solution)/shard_map/ppermute | solution.py:36
  127.6 1.5 collective-permute-start.14
  127.7 1.7 collective-permute-start.15
  138.7 11.3 %collective-permute-start.16 = (f32[2,3,16,1024]{3,2,1,0:T(8,128)S(1)}, f32[2,3,16,1024]{3,2,1,0:T(8,128)S(1)}, u32[]{:S(2)}, u32[]{:S(2)}) collective-permute-start(f32[2,3,16,1024]{3,2,1,0:T(8,128)S(1)} %broadcast_select_fusion), channel_id=1, source_target_pairs={{0,2},{2,0},{4,6},{6,4},{8,10},{10,8},{12,14},{14,12},{16,18},{18,... | collective-permute-start | bytes 1179656 | tf_op jit(solution)/shard_map/ppermute | solution.py:36
  150.2 10.5 %collective-permute-start.17 = (f32[2,3,16,1024]{3,2,1,0:T(8,128)S(1)}, f32[2,3,16,1024]{3,2,1,0:T(8,128)S(1)}, u32[]{:S(2)}, u32[]{:S(2)}) collective-permute-start(f32[2,3,16,1024]{3,2,1,0:T(8,128)S(1)} %broadcast_select_fusion.11), channel_id=1, source_target_pairs={{0,4},{4,0},{2,6},{6,2},{8,12},{12,8},{10,14},{14,10},{16,20},{20,... | collective-permute-start | bytes 1179656 | tf_op jit(solution)/shard_map/ppermute | solution.py:36
  160.8 9.6 %collective-permute-start.18 = (f32[2,3,16,1024]{3,2,1,0:T(8,128)S(1)}, f32[2,3,16,1024]{3,2,1,0:T(8,128)S(1)}, u32[]{:S(2)}, u32[]{:S(2)}) collective-permute-start(f32[2,3,16,1024]{3,2,1,0:T(8,128)S(1)} %broadcast_select_fusion.12), channel_id=1, source_target_pairs={{0,8},{8,0},{2,10},{10,2},{4,12},{12,4},{6,14},{14,6},{16,24},{24,... | collective-permute-start | bytes 1179656 | tf_op jit(solution)/shard_map/ppermute | solution.py:36
  170.5 18.0 %collective-permute-start.19 = (f32[2,3,16,1024]{3,2,1,0:T(8,128)S(1)}, f32[2,3,16,1024]{3,2,1,0:T(8,128)S(1)}, u32[]{:S(2)}, u32[]{:S(2)}) collective-permute-start(f32[2,3,16,1024]{3,2,1,0:T(8,128)S(1)} %broadcast_select_fusion.13), channel_id=1, source_target_pairs={{0,16},{16,0},{2,18},{18,2},{4,20},{20,4},{6,22},{22,6},{8,24},{24... | collective-permute-start | bytes 1179656 | tf_op jit(solution)/shard_map/ppermute | solution.py:36
where the time goes:
time: 190 us; the launch traced here: 189 us
  waiting for transfers between devices  135 us (71%)
  starting transfers between devices  19.7 us (10%)
  other arithmetic  17.3 us (9%)
  local copies, waits for them, and re-layouts  16 us (8%)
    ppermute x12, waiting for transfers between devices, partner(): return lax.ppermute(block, axis, route)  132 us
    ppermute x12, starting transfers between devices, partner(): return lax.ppermute(block, axis, route)  17.4 us
    another operation x47, other arithmetic, rates(): return jnp.stack([rate_h, rate_u, rate_v], 1)  8.01 us
    slice x48, local copies, waits for them, and re-layouts, rates(): slope_x = (jnp.roll(height, -1, -1) - jnp.roll(height, 1, -1))[:, 1:-1]  4.68 us
    slice x48, local copies, waits for them, and re-layouts, rates(): diff_x = (jnp.roll(flux_x, -1, -1) - jnp.roll(flux_x, 1, -1))[:, 1:-1]  4.67 us
  transfers between devices with their start and end apart: 20, of which 16 were waited for; matrix products, arithmetic and copies ran while one was open for 1% of the time, Pallas kernels for 0%

commit v1 on v0

v1 whole, which is shorter than its diff:
```python
import functools

import jax
import jax.numpy as jnp
from jax import lax
from jax.experimental import pallas as pl
from jax.experimental.pallas import tpu as pltpu
from jax.sharding import PartitionSpec as P

STEPS = 4
CYCLES = 3


gravity = 2.0
coriolis = 0.1
friction = 0.02
time_step = 0.25

LANES = 128
SUBLANES = 8
MESH = pl.DeviceIdType.MESH


def extended(x, sides, width):
    for axis, dim in sides:
        devices, length = (lax.axis_size(axis), x.shape[dim])
        up = [(i, (i + 1) % devices) for i in range(devices)]
        down = [(j, i) for i, j in up]
        last = lax.slice_in_dim(x, length - width, length, axis=dim)
        leading = lax.slice_in_dim(x, 0, width, axis=dim)
        before = lax.ppermute(last, axis, up)
        after = lax.ppermute(leading, axis, down)
        x = jnp.concatenate([before, x, after], axis=dim)
    return x


def rates(padded, depth_pad):
    height = padded[:, 0]
    east = padded[:, 1]
    north = padded[:, 2]
    column = depth_pad + height
    flux_x = column * east
    flux_y = column * north
    diff_x = (jnp.roll(flux_x, -1, -1) - jnp.roll(flux_x, 1, -1))[:, 1:-1]
    diff_y = flux_y[:, 2:] - flux_y[:, :-2]
    rate_h = -0.5 * (diff_x + diff_y)
    slope_x = (jnp.roll(height, -1, -1) - jnp.roll(height, 1, -1))[:, 1:-1]
    slope_y = height[:, 2:] - height[:, :-2]
    east_mid = east[:, 1:-1]
    north_mid = north[:, 1:-1]
    rate_u = -0.5 * gravity * slope_x + coriolis * north_mid - friction * east_mid
    rate_v = -0.5 * gravity * slope_y - coriolis * east_mid - friction * north_mid
    return jnp.stack([rate_h, rate_u, rate_v], 1)


def trim_depth(depth_full, width):
    offset = 2 * STEPS - width
    total = depth_full.shape[0]
    return depth_full[offset : total - offset]


def general_body(fields, bathymetry, copy_lists):
    depth_ext = extended(bathymetry, (("row", 0),), 2 * STEPS)
    depth_full = depth_ext.astype(jnp.float32) / 100.0
    current = fields
    for _ in range(CYCLES):
        padded = extended(current, (("row", 2),), 2 * STEPS)
        for step_no in range(STEPS):
            width = 2 * (STEPS - step_no)
            first_rate = rates(padded, trim_depth(depth_full, width))
            rows_now = padded.shape[2]
            middle = padded[:, :, 1 : rows_now - 1] + time_step * first_rate
            second_rate = rates(middle, trim_depth(depth_full, width - 1))
            rows_mid = first_rate.shape[2]
            padded = padded[:, :, 2 : rows_now - 2] + 0.5 * time_step * (
                first_rate[:, :, 1 : rows_mid - 1] + second_rate
            )
        current = padded
    sources = jnp.arange(copy_lists.shape[2], dtype=jnp.int32)
    for cycle_no in reversed(range(copy_lists.shape[0])):
        for section_no in reversed(range(copy_lists.shape[1])):
            sources = jnp.take(copy_lists[cycle_no, section_no], sources)
    spread = lax.all_to_all(current, "member", split_axis=3, concat_axis=0, tiled=True)
    return lax.all_to_all(
        jnp.take(spread, sources, axis=0), "member", split_axis=0, concat_axis=3, tiled=True
    )


def advance(state, flux, depth, target, target_flux, base, scale, col, rows, lane):
    cols = state.shape[2] // LANES
    here = pl.ds(col * LANES, LANES)
    left = pl.ds((col - 1) % cols * LANES, LANES)
    right = pl.ds((col + 1) % cols * LANES, LANES)

    def from_left(ref):
        return pltpu.roll(jnp.where(lane == LANES - 1, ref[:, left], ref[:, here]), 1, 1)

    def from_right(ref):
        return pltpu.roll(jnp.where(lane == 0, ref[:, right], ref[:, here]), LANES - 1, 1)

    height = state[0, :, here]
    east = state[1, :, here]
    north = state[2, :, here]
    rest = depth[:, here]
    flux_y = (rest + height) * north
    diff_x = from_right(flux) - from_left(flux)
    diff_y = pltpu.roll(flux_y, rows - 1, 0) - pltpu.roll(flux_y, 1, 0)
    slope_x = from_right(state.at[0]) - from_left(state.at[0])
    slope_y = pltpu.roll(height, rows - 1, 0) - pltpu.roll(height, 1, 0)
    keep = 1.0 if base is None else 0.5
    drag = keep - scale * friction
    turn = scale * coriolis
    push = 0.5 * gravity * scale
    new_h = (height if base is None else 0.5 * height) - (0.5 * scale) * (diff_x + diff_y)
    new_u = drag * east + turn * north - push * slope_x
    new_v = drag * north - turn * east - push * slope_y
    if base is not None:
        new_h = new_h + 0.5 * base[0, :, here]
        new_u = new_u + 0.5 * base[1, :, here]
        new_v = new_v + 0.5 * base[2, :, here]
    target[0, :, here] = new_h
    target[1, :, here] = new_u
    target[2, :, here] = new_v
    target_flux[:, here] = (rest + new_h) * new_u


def kernel(
    members_axis, rows_axis, fields, bathymetry, lists, out,
    state, middle, flux, flux_mid, resting, depth, held, picked, sources,
    load_sem, swap_send, swap_recv, spread_send, spread_recv, back_send, back_recv,
):
    group, row_no = lax.axis_index("member"), lax.axis_index("row")
    devices = members_axis * rows_axis
    me = group * rows_axis + row_no
    tile_rows, width = fields.shape[2], fields.shape[3]
    rows = tile_rows * rows_axis
    cols = width // LANES
    local = fields.shape[0]
    part = held.shape[2]
    own_rows = pl.ds(pl.multiple_of(row_no * tile_rows, SUBLANES), tile_rows)

    own_fields = pltpu.make_async_copy(fields.at[row_no], state.at[:, own_rows], load_sem.at[0])
    own_depth = pltpu.make_async_copy(bathymetry, resting.at[own_rows], load_sem.at[1])
    own_fields.start()
    own_depth.start()

    barrier = pltpu.get_barrier_semaphore()

    def greet(k, carry):
        other = lax.rem(me + k, devices)
        pl.semaphore_signal(
            barrier, inc=1, device_id=(other // rows_axis, lax.rem(other, rows_axis)),
            device_id_type=MESH,
        )
        return carry

    lax.fori_loop(1, devices, greet, 0)
    pl.semaphore_wait(barrier, devices - 1)

    swaps = []
    for k in range(1, rows_axis):
        other = lax.rem(row_no + k, rows_axis)
        for n, (src, dst) in enumerate(
            ((bathymetry, resting.at[own_rows]), (fields.at[other], state.at[:, own_rows]))
        ):
            copy = pltpu.make_async_remote_copy(
                src_ref=src, dst_ref=dst,
                send_sem=swap_send.at[2 * k + n], recv_sem=swap_recv.at[2 * k + n],
                device_id=(group, other), device_id_type=MESH,
            )
            copy.start()
            swaps.append(copy)
    own_fields.wait()
    own_depth.wait()
    for copy in swaps:
        copy.wait()

    depth[...] = resting[...].astype(jnp.float32) / 100.0
    flux[...] = (depth[...] + state[0]) * state[1]
    lane = lax.broadcasted_iota(jnp.int32, (rows, LANES), 1)

    def step(_, carry):
        for col in range(cols):
            advance(state, flux, depth, middle, flux_mid, None, time_step, col, rows, lane)
        for col in range(cols):
            advance(middle, flux_mid, depth, state, flux, state, 0.5 * time_step, col, rows, lane)
        return carry

    lax.fori_loop(0, STEPS * CYCLES, step, 0)

    def piece(j, r):
        return state.at[
            :,
            pl.ds(pl.multiple_of(r * tile_rows + j // cols * part, SUBLANES), part),
            pl.ds(pl.multiple_of(lax.rem(j, cols) * LANES, LANES), LANES),
        ]

    def spread_copy(k):
        other = lax.rem(me + k, devices)
        j, r = other // rows_axis, lax.rem(other, rows_axis)
        return pltpu.make_async_remote_copy(
            src_ref=piece(j, r), dst_ref=held.at[me],
            send_sem=spread_send.at[k], recv_sem=spread_recv,
            device_id=(j, r), device_id_type=MESH,
        )

    def start_spread(k, carry):
        spread_copy(k).start()
        return carry

    lax.fori_loop(1, devices, start_spread, 0)
    pltpu.make_async_copy(piece(group, row_no), held.at[me], spread_recv).start()

    def compose(m, carry):
        source = m
        for cycle_no in reversed(range(lists.shape[0])):
            for section_no in reversed(range(lists.shape[1])):
                source = lists[cycle_no, section_no, source]
        sources[m] = source
        return carry

    lax.fori_loop(0, held.shape[0], compose, 0)
    pltpu.make_async_copy(held, held, spread_recv).wait()

    for m in range(held.shape[0]):
        picked[m] = held[sources[m]]

    place = out.at[
        :,
        :,
        pl.ds(pl.multiple_of(group // cols * part, SUBLANES), part),
        pl.ds(pl.multiple_of(lax.rem(group, cols) * LANES, LANES), LANES),
    ]

    def back_copy(k):
        other = lax.rem(group + k, members_axis)
        return pltpu.make_async_remote_copy(
            src_ref=picked.at[pl.ds(other * local, local)], dst_ref=place,
            send_sem=back_send.at[k], recv_sem=back_recv,
            device_id=(other, row_no), device_id_type=MESH,
        )

    def start_back(k, carry):
        back_copy(k).start()
        return carry

    lax.fori_loop(1, members_axis, start_back, 0)
    pltpu.make_async_copy(picked.at[pl.ds(group * local, local)], place, back_recv).start()

    def end_spread(k, carry):
        spread_copy(k).wait_send()
        return carry

    lax.fori_loop(1, devices, end_spread, 0)

    def end_back(k, carry):
        back_copy(k).wait_send()
        return carry

    lax.fori_loop(1, members_axis, end_back, 0)
    pltpu.make_async_copy(out, out, back_recv).wait()


def fast_body(members_axis, rows_axis, fields, bathymetry, copy_lists):
    local, kinds, tile_rows, width = fields.shape
    rows = tile_rows * rows_axis
    part = tile_rows // (members_axis // (width // LANES))
    f32 = jnp.float32
    dma = pltpu.SemaphoreType.DMA
    return pl.pallas_call(
        functools.partial(kernel, members_axis, rows_axis),
        out_shape=jax.ShapeDtypeStruct(fields.shape, f32),
        in_specs=[
            pl.BlockSpec(memory_space=pl.ANY),
            pl.BlockSpec(memory_space=pl.ANY),
            pl.BlockSpec(memory_space=pltpu.SMEM),
        ],
        out_specs=pl.BlockSpec(memory_space=pltpu.VMEM),
        scratch_shapes=[
            pltpu.VMEM((kinds, rows, width), f32),
            pltpu.VMEM((kinds, rows, width), f32),
            pltpu.VMEM((rows, width), f32),
            pltpu.VMEM((rows, width), f32),
            pltpu.VMEM((rows, width), jnp.int32),
            pltpu.VMEM((rows, width), f32),
            pltpu.VMEM((members_axis * local, kinds, part, LANES), f32),
            pltpu.VMEM((members_axis * local, kinds, part, LANES), f32),
            pltpu.SMEM((members_axis * local,), jnp.int32),
            dma((2,)),
            dma((2 * rows_axis,)),
            dma((2 * rows_axis,)),
            dma((members_axis * rows_axis,)),
            dma,
            dma((members_axis,)),
            dma,
        ],
        compiler_params=pltpu.CompilerParams(
            collective_id=0, has_side_effects=True, vmem_limit_bytes=32 * 1024 * 1024
        ),
    )(fields, bathymetry, copy_lists)


def solution(mesh):
    members_axis, rows_axis = mesh.shape["member"], mesh.shape["row"]
    placed = (P("member", None, "row", None), P("row", None), P())

    def body(fields, bathymetry, copy_lists):
        local, _, tile_rows, width = fields.shape
        cols = width // LANES
        splits = max(members_axis // cols, 1)
        fits = (
            local == rows_axis
            and width % LANES == 0
            and members_axis % cols == 0
            and tile_rows % (splits * SUBLANES) == 0
        )
        if fits:
            return fast_body(members_axis, rows_axis, fields, bathymetry, copy_lists)
        return general_body(fields, bathymetry, copy_lists)

    return jax.shard_map(
        body, mesh=mesh, in_specs=placed, out_specs=P("member", None, "row", None), check_vma=False
    )
```

time: 190 us -> 37.1 us (0.20)
  the two profiles are of different devices: /device:TPU:0 before, /device:TPU:28 now
where the time goes in v1:
time: 37.1 us; the launch traced here: 36.9 us
  Pallas kernels  33.6 us (91%)
  local copies, waits for them, and re-layouts  3.29 us (9%)
    pallas_call x1, Pallas kernels, fast_body(): pl.pallas_call(functools.partial(kernel, members_axis, rows_axis), out_sh...  33.6 us
    unnamed x6, local copies, waits for them, and re-layouts  3.29 us

profile of v1, /device:TPU:28, one launch (start us, length us, event | category | flops | bytes accessed | tf_op | source)
XLA Modules:
  0.0 36.9 jit_solution(8786977266408292638)
XLA Ops:
  0.0 0.7 %copy.4.lists = s32[3,5,32]{2,1,0:T(8,128)S(1)} copy(s32[3,5,32]{2,0,1:T(4,128)} %param.5) | data formatting | bytes 3840 | tf_op args[2]
  0.7 0.0 copy-start
  0.7 1.0 %copy-done = f32[2,3,16,1024]{3,2,1,0:T(8,128)S(1)} copy-done((f32[2,3,16,1024]{3,2,1,0:T(8,128)S(1)}, f32[2,3,16,1024]{3,2,1,0:T(8,128)}, u32[]{:S(2)}) %copy-start) | copy-done | bytes 393240
  1.7 0.0 copy-start.1
  1.7 0.8 %copy-done.1 = s32[16,1024]{1,0:T(8,128)S(1)} copy-done((s32[16,1024]{1,0:T(8,128)S(1)}, s32[16,1024]{1,0:T(8,128)}, u32[]{:S(2)}) %copy-start.1) | copy-done | bytes 65560
  2.5 33.6 %shard_map.37 = f32[2,3,16,1024]{3,2,1,0:T(8,128)S(1)} custom-call(f32[2,3,16,1024]{3,2,1,0:T(8,128)S(1)} %copy-done, s32[16,1024]{1,0:T(8,128)S(1)} %copy-done.1, s32[3,5,32]{2,1,0:T(8,128)S(1)} %copy.4.lists), custom_call_target="tpu_custom_call" | custom-call | tf_op jit(solution)/shard_map/pallas_call | solution.py:270
  36.1 0.7 %copy.6 = f32[2,3,16,1024]{3,2,1,0:T(8,128)} copy(f32[2,3,16,1024]{3,2,1,0:T(8,128)S(1)} %shard_map.37) | data formatting | bytes 786432
Async XLA Ops:
  0.7 1.0 %copy-start = (f32[2,3,16,1024]{3,2,1,0:T(8,128)S(1)}, f32[2,3,16,1024]{3,2,1,0:T(8,128)}, u32[]{:S(2)}) copy-start(f32[2,3,16,1024]{3,2,1,0:T(8,128)} %fields.1) | copy-start | bytes 1179652
  1.7 0.8 %copy-start.1 = (s32[16,1024]{1,0:T(8,128)S(1)}, s32[16,1024]{1,0:T(8,128)}, u32[]{:S(2)}) copy-start(s32[16,1024]{1,0:T(8,128)} %bathymetry.1) | copy-start | bytes 196612

commit v2 on v1

--- a/solution.py
+++ b/solution.py
@@ -195,27 +195,34 @@
             pl.ds(pl.multiple_of(lax.rem(j, cols) * LANES, LANES), LANES),
         ]
 
-    def spread_copy(k):
-        other = lax.rem(me + k, devices)
+    def spread_copy(other):
         j, r = other // rows_axis, lax.rem(other, rows_axis)
         return pltpu.make_async_remote_copy(
             src_ref=piece(j, r), dst_ref=held.at[me],
-            send_sem=spread_send.at[k], recv_sem=spread_recv,
+            send_sem=spread_send.at[other], recv_sem=spread_recv,
             device_id=(j, r), device_id_type=MESH,
         )
 
-    def start_spread(k, carry):
-        spread_copy(k).start()
-        return carry
-
-    lax.fori_loop(1, devices, start_spread, 0)
+    half = devices // 2
+    side, seat = me // half, lax.rem(me, half)
+
+    def start_far(k, carry):
+        spread_copy((1 - side) * half + lax.rem(seat + k, half)).start()
+        return carry
+
+    def start_near(k, carry):
+        spread_copy(side * half + lax.rem(seat + k, half)).start()
+        return carry
+
+    lax.fori_loop(0, half, start_far, 0)
+    lax.fori_loop(1, half, start_near, 0)
     pltpu.make_async_copy(piece(group, row_no), held.at[me], spread_recv).start()
 
     def compose(m, carry):
         source = m
-        for cycle_no in reversed(range(lists.shape[0])):
-            for section_no in reversed(range(lists.shape[1])):
-                source = lists[cycle_no, section_no, source]
+        for cycle_no in reversed(range(lists.shape[1])):
+            for section_no in reversed(range(lists.shape[0])):
+                source = lists[section_no, cycle_no, source]
         sources[m] = source
         return carry
 
@@ -240,15 +247,18 @@
             device_id=(other, row_no), device_id_type=MESH,
         )
 
+    back_half = members_axis // 2
+
     def start_back(k, carry):
-        back_copy(k).start()
-        return carry
-
-    lax.fori_loop(1, members_axis, start_back, 0)
+        back_copy(lax.rem(back_half + k, members_axis)).start()
+        return carry
+
+    lax.fori_loop(0, back_half, start_back, 0)
+    lax.fori_loop(back_half + 1, members_axis, start_back, 0)
     pltpu.make_async_copy(picked.at[pl.ds(group * local, local)], place, back_recv).start()
 
     def end_spread(k, carry):
-        spread_copy(k).wait_send()
+        spread_copy(lax.rem(me + k, devices)).wait_send()
         return carry
 
     lax.fori_loop(1, devices, end_spread, 0)
@@ -271,8 +281,8 @@
         functools.partial(kernel, members_axis, rows_axis),
         out_shape=jax.ShapeDtypeStruct(fields.shape, f32),
         in_specs=[
-            pl.BlockSpec(memory_space=pl.ANY),
-            pl.BlockSpec(memory_space=pl.ANY),
+            pl.BlockSpec(memory_space=pltpu.HBM),
+            pl.BlockSpec(memory_space=pltpu.HBM),
             pl.BlockSpec(memory_space=pltpu.SMEM),
         ],
         out_specs=pl.BlockSpec(memory_space=pltpu.VMEM),
@@ -297,7 +307,7 @@
         compiler_params=pltpu.CompilerParams(
             collective_id=0, has_side_effects=True, vmem_limit_bytes=32 * 1024 * 1024
         ),
-    )(fields, bathymetry, copy_lists)
+    )(fields, bathymetry, jnp.swapaxes(copy_lists, 0, 1))
 
 
 def solution(mesh):
@@ -312,6 +322,7 @@
             local == rows_axis
             and width % LANES == 0
             and members_axis % cols == 0
+            and members_axis % 2 == 0
             and tile_rows % (splits * SUBLANES) == 0
         )
         if fits:

time: 37.1 us -> 40.2 us (1.084)
  the two profiles are of different devices: /device:TPU:28 before, /device:TPU:0 now
where the time goes in v2:
time: 40.2 us; the launch traced here: 39.9 us
  Pallas kernels  36.6 us (91%)
  local copies, waits for them, and re-layouts  3.28 us (8%)
    pallas_call x1, Pallas kernels, fast_body(): pl.pallas_call(functools.partial(kernel, members_axis, rows_axis), out_sh...  36.6 us
    unnamed x7, local copies, waits for them, and re-layouts  3.28 us

profile of v2, /device:TPU:0, one launch (start us, length us, event | category | flops | bytes accessed | tf_op | source)
XLA Modules:
  0.0 39.9 jit_solution(4887829906178223266)
XLA Ops:
  0.0 0.0 copy-start
  0.0 1.0 %copy-done = f32[2,3,16,1024]{3,2,1,0:T(8,128)S(1)} copy-done((f32[2,3,16,1024]{3,2,1,0:T(8,128)S(1)}, f32[2,3,16,1024]{3,2,1,0:T(8,128)}, u32[]{:S(2)}) %copy-start) | copy-done | bytes 393240
  1.0 0.0 copy-start.1
  1.0 0.8 %copy-done.1 = s32[16,1024]{1,0:T(8,128)S(1)} copy-done((s32[16,1024]{1,0:T(8,128)S(1)}, s32[16,1024]{1,0:T(8,128)}, u32[]{:S(2)}) %copy-start.1) | copy-done | bytes 65560
  1.8 0.0 copy-start.2
  1.8 0.7 %copy-done.2 = s32[3,5,32]{2,0,1:T(4,128)S(1)} copy-done((s32[3,5,32]{2,0,1:T(4,128)S(1)}, s32[3,5,32]{2,0,1:T(4,128)}, u32[]{:S(2)}) %copy-start.2) | copy-done | bytes 1944
  2.5 36.6 %shard_map.37 = f32[2,3,16,1024]{3,2,1,0:T(8,128)S(1)} custom-call(f32[2,3,16,1024]{3,2,1,0:T(8,128)S(1)} %copy-done, s32[16,1024]{1,0:T(8,128)S(1)} %copy-done.1, s32[5,3,32]{2,1,0:T(4,128)S(1)} %bitcast.1), custom_call_target="tpu_custom_call" | custom-call | tf_op jit(solution)/shard_map/pallas_call | solution.py:280
  39.2 0.7 %copy.5 = f32[2,3,16,1024]{3,2,1,0:T(8,128)} copy(f32[2,3,16,1024]{3,2,1,0:T(8,128)S(1)} %shard_map.37) | data formatting | bytes 786432
Async XLA Ops:
  0.0 1.0 %copy-start = (f32[2,3,16,1024]{3,2,1,0:T(8,128)S(1)}, f32[2,3,16,1024]{3,2,1,0:T(8,128)}, u32[]{:S(2)}) copy-start(f32[2,3,16,1024]{3,2,1,0:T(8,128)} %fields.1) | copy-start | bytes 1179652
  1.0 0.8 %copy-start.1 = (s32[16,1024]{1,0:T(8,128)S(1)}, s32[16,1024]{1,0:T(8,128)}, u32[]{:S(2)}) copy-start(s32[16,1024]{1,0:T(8,128)} %bathymetry.1) | copy-start | bytes 196612
  1.8 0.7 %copy-start.2 = (s32[3,5,32]{2,0,1:T(4,128)S(1)}, s32[3,5,32]{2,0,1:T(4,128)}, u32[]{:S(2)}) copy-start(s32[3,5,32]{2,0,1:T(4,128)} %param.5) | copy-start | bytes 5764

commit v3 on v2

--- a/solution.py
+++ b/solution.py
@@ -125,8 +125,8 @@
 
 
 def kernel(
-    members_axis, rows_axis, fields, bathymetry, lists, out,
-    state, middle, flux, flux_mid, resting, depth, held, picked, sources,
+    members_axis, rows_axis, fields, bathymetry, lists_in, out,
+    state, middle, flux, flux_mid, resting, depth, held, picked, lists, sources,
     load_sem, swap_send, swap_recv, spread_send, spread_recv, back_send, back_recv,
 ):
     group, row_no = lax.axis_index("member"), lax.axis_index("row")
@@ -136,13 +136,15 @@
     rows = tile_rows * rows_axis
     cols = width // LANES
     local = fields.shape[0]
-    part = held.shape[2]
+    part = held[0].shape[1]
     own_rows = pl.ds(pl.multiple_of(row_no * tile_rows, SUBLANES), tile_rows)
 
     own_fields = pltpu.make_async_copy(fields.at[row_no], state.at[:, own_rows], load_sem.at[0])
     own_depth = pltpu.make_async_copy(bathymetry, resting.at[own_rows], load_sem.at[1])
+    own_lists = pltpu.make_async_copy(lists_in, lists, load_sem.at[2])
     own_fields.start()
     own_depth.start()
+    own_lists.start()
 
     barrier = pltpu.get_barrier_semaphore()
 
@@ -188,35 +190,41 @@
 
     lax.fori_loop(0, STEPS * CYCLES, step, 0)
 
-    def piece(j, r):
+    def piece(kind, j, r):
         return state.at[
-            :,
+            kind,
             pl.ds(pl.multiple_of(r * tile_rows + j // cols * part, SUBLANES), part),
             pl.ds(pl.multiple_of(lax.rem(j, cols) * LANES, LANES), LANES),
         ]
 
-    def spread_copy(other):
+    def spread_copy(kind, other):
         j, r = other // rows_axis, lax.rem(other, rows_axis)
         return pltpu.make_async_remote_copy(
-            src_ref=piece(j, r), dst_ref=held.at[me],
-            send_sem=spread_send.at[other], recv_sem=spread_recv,
+            src_ref=piece(kind, j, r), dst_ref=held[kind].at[me],
+            send_sem=spread_send.at[kind, other], recv_sem=spread_recv.at[kind],
             device_id=(j, r), device_id_type=MESH,
         )
 
     half = devices // 2
     side, seat = me // half, lax.rem(me, half)
-
-    def start_far(k, carry):
-        spread_copy((1 - side) * half + lax.rem(seat + k, half)).start()
-        return carry
-
-    def start_near(k, carry):
-        spread_copy(side * half + lax.rem(seat + k, half)).start()
-        return carry
-
-    lax.fori_loop(0, half, start_far, 0)
-    lax.fori_loop(1, half, start_near, 0)
-    pltpu.make_async_copy(piece(group, row_no), held.at[me], spread_recv).start()
+    far, near = (1 - side) * half, side * half
+    kinds = state.shape[0]
+
+    for kind in range(kinds):
+        spread_copy(kind, far + seat).start()
+
+        def start_spread(k, carry, kind=kind):
+            there = lax.rem(seat + k, half)
+            spread_copy(kind, far + there).start()
+            spread_copy(kind, near + there).start()
+            return carry
+
+        lax.fori_loop(1, half, start_spread, 0)
+        pltpu.make_async_copy(
+            piece(kind, group, row_no), held[kind].at[me], spread_recv.at[kind]
+        ).start()
+
+    own_lists.wait()
 
     def compose(m, carry):
         source = m
@@ -226,49 +234,59 @@
         sources[m] = source
         return carry
 
-    lax.fori_loop(0, held.shape[0], compose, 0)
-    pltpu.make_async_copy(held, held, spread_recv).wait()
-
-    for m in range(held.shape[0]):
-        picked[m] = held[sources[m]]
-
-    place = out.at[
-        :,
-        :,
-        pl.ds(pl.multiple_of(group // cols * part, SUBLANES), part),
-        pl.ds(pl.multiple_of(lax.rem(group, cols) * LANES, LANES), LANES),
-    ]
-
-    def back_copy(k):
-        other = lax.rem(group + k, members_axis)
+    lax.fori_loop(0, sources.shape[0], compose, 0)
+
+    def place(kind):
+        return out.at[
+            :,
+            kind,
+            pl.ds(pl.multiple_of(group // cols * part, SUBLANES), part),
+            pl.ds(pl.multiple_of(lax.rem(group, cols) * LANES, LANES), LANES),
+        ]
+
+    def back_copy(kind, other):
         return pltpu.make_async_remote_copy(
-            src_ref=picked.at[pl.ds(other * local, local)], dst_ref=place,
-            send_sem=back_send.at[k], recv_sem=back_recv,
+            src_ref=picked[kind].at[pl.ds(other * local, local)], dst_ref=place(kind),
+            send_sem=back_send.at[kind, other], recv_sem=back_recv.at[kind],
             device_id=(other, row_no), device_id_type=MESH,
         )
 
     back_half = members_axis // 2
-
-    def start_back(k, carry):
-        back_copy(lax.rem(back_half + k, members_axis)).start()
-        return carry
-
-    lax.fori_loop(0, back_half, start_back, 0)
-    lax.fori_loop(back_half + 1, members_axis, start_back, 0)
-    pltpu.make_async_copy(picked.at[pl.ds(group * local, local)], place, back_recv).start()
-
-    def end_spread(k, carry):
-        spread_copy(lax.rem(me + k, devices)).wait_send()
-        return carry
-
-    lax.fori_loop(1, devices, end_spread, 0)
-
-    def end_back(k, carry):
-        back_copy(k).wait_send()
-        return carry
-
-    lax.fori_loop(1, members_axis, end_back, 0)
-    pltpu.make_async_copy(out, out, back_recv).wait()
+    back_side, back_seat = group // back_half, lax.rem(group, back_half)
+    back_far, back_near = (1 - back_side) * back_half, back_side * back_half
+
+    for kind in range(kinds):
+        pltpu.make_async_copy(held[kind], held[kind], spread_recv.at[kind]).wait()
+        for m in range(sources.shape[0]):
+            picked[kind][m] = held[kind][sources[m]]
+        back_copy(kind, back_far + back_seat).start()
+
+        def start_back(k, carry, kind=kind):
+            there = lax.rem(back_seat + k, back_half)
+            back_copy(kind, back_far + there).start()
+            back_copy(kind, back_near + there).start()
+            return carry
+
+        lax.fori_loop(1, back_half, start_back, 0)
+        pltpu.make_async_copy(
+            picked[kind].at[pl.ds(group * local, local)], place(kind), back_recv.at[kind]
+        ).start()
+
+    for kind in range(kinds):
+
+        def end_spread(k, carry, kind=kind):
+            spread_copy(kind, lax.rem(me + k, devices)).wait_send()
+            return carry
+
+        lax.fori_loop(1, devices, end_spread, 0)
+
+        def end_back(k, carry, kind=kind):
+            back_copy(kind, lax.rem(group + k, members_axis)).wait_send()
+            return carry
+
+        lax.fori_loop(1, members_axis, end_back, 0)
+    for kind in range(kinds):
+        pltpu.make_async_copy(out.at[:, kind], out.at[:, kind], back_recv.at[kind]).wait()
 
 
 def fast_body(members_axis, rows_axis, fields, bathymetry, copy_lists):
@@ -283,7 +301,7 @@
         in_specs=[
             pl.BlockSpec(memory_space=pltpu.HBM),
             pl.BlockSpec(memory_space=pltpu.HBM),
-            pl.BlockSpec(memory_space=pltpu.SMEM),
+            pl.BlockSpec(memory_space=pltpu.HBM),
         ],
         out_specs=pl.BlockSpec(memory_space=pltpu.VMEM),
         scratch_shapes=[
@@ -293,19 +311,20 @@
             pltpu.VMEM((rows, width), f32),
             pltpu.VMEM((rows, width), jnp.int32),
             pltpu.VMEM((rows, width), f32),
-            pltpu.VMEM((members_axis * local, kinds, part, LANES), f32),
-            pltpu.VMEM((members_axis * local, kinds, part, LANES), f32),
+            [pltpu.VMEM((members_axis * local, part, LANES), f32)] * kinds,
+            [pltpu.VMEM((members_axis * local, part, LANES), f32)] * kinds,
+            pltpu.SMEM((copy_lists.shape[1], copy_lists.shape[0], copy_lists.shape[2]), jnp.int32),
             pltpu.SMEM((members_axis * local,), jnp.int32),
-            dma((2,)),
+            dma((3,)),
             dma((2 * rows_axis,)),
             dma((2 * rows_axis,)),
-            dma((members_axis * rows_axis,)),
-            dma,
-            dma((members_axis,)),
-            dma,
+            dma((kinds, members_axis * rows_axis)),
+            dma((kinds,)),
+            dma((kinds, members_axis)),
+            dma((kinds,)),
         ],
         compiler_params=pltpu.CompilerParams(
-            collective_id=0, has_side_effects=True, vmem_limit_bytes=32 * 1024 * 1024
+            collective_id=0, has_side_effects=True
         ),
     )(fields, bathymetry, jnp.swapaxes(copy_lists, 0, 1))
 

time: 40.2 us -> 36.5 us (0.908)
  Pallas kernels: 36.6 us -> 34.6 us
  local copies, waits for them, and re-layouts: 3.28 us -> 1.77 us
    pallas_call x1, Pallas kernels: 36.6 us -> 34.6 us  [fast_body(): pl.pallas_call(functools.partial(kernel, members_axis, rows_axis), out_sh...]
    unnamed x7 -> x1, local copies, waits for them, and re-layouts: 3.28 us -> 1.77 us
where the time goes in v3:
time: 36.5 us; the launch traced here: 36.4 us
  Pallas kernels  34.6 us (95%)
  local copies, waits for them, and re-layouts  1.77 us (5%)
    pallas_call x1, Pallas kernels, fast_body(): pl.pallas_call(functools.partial(kernel, members_axis, rows_axis), out_sh...  34.6 us
    unnamed x1, local copies, waits for them, and re-layouts  1.77 us

profile of v3, /device:TPU:0, one launch (start us, length us, event | category | flops | bytes accessed | tf_op | source)
XLA Modules:
  0.0 36.4 jit_solution(14773858255621363318)
XLA Ops:
  0.0 34.6 %shard_map.37 = f32[2,3,16,1024]{3,2,1,0:T(8,128)} custom-call(f32[2,3,16,1024]{3,2,1,0:T(8,128)} %fields.1, s32[16,1024]{1,0:T(8,128)} %bathymetry.1, s32[5,3,32]{2,1,0:T(4,128)} %bitcast.1), custom_call_target="tpu_custom_call" | custom-call | tf_op jit(solution)/shard_map/pallas_call | solution.py:298
  34.6 1.8 %copy.5 = f32[2,3,16,1024]{3,2,1,0:T(8,128)} copy(f32[2,3,16,1024]{3,2,1,0:T(8,128)} %shard_map.37) | data formatting | bytes 786432

commit v4 on v1

--- a/solution.py
+++ b/solution.py
@@ -19,6 +19,7 @@
 LANES = 128
 SUBLANES = 8
 MESH = pl.DeviceIdType.MESH
+LAG = 2
 
 
 def extended(x, sides, width):
@@ -124,25 +125,34 @@
     target_flux[:, here] = (rest + new_h) * new_u
 
 
+def alternate(count):
+    half = count // 2
+    return [k for pair in zip(range(half, count), [*range(1, half), 0]) for k in pair]
+
+
 def kernel(
-    members_axis, rows_axis, fields, bathymetry, lists, out,
-    state, middle, flux, flux_mid, resting, depth, held, picked, sources,
+    members_axis, rows_axis, fields, bathymetry, lists_in, out,
+    state, resting, work, middle, flux, flux_mid, depth, held, picked, lists, sources,
     load_sem, swap_send, swap_recv, spread_send, spread_recv, back_send, back_recv,
 ):
     group, row_no = lax.axis_index("member"), lax.axis_index("row")
     devices = members_axis * rows_axis
     me = group * rows_axis + row_no
-    tile_rows, width = fields.shape[2], fields.shape[3]
+    local, kinds, tile_rows, width = fields.shape
     rows = tile_rows * rows_axis
     cols = width // LANES
-    local = fields.shape[0]
-    part = held.shape[2]
+    chunks = work.shape[0]
+    chunk_cols = cols // chunks
+    per_chunk = members_axis // 2
+    members = members_axis * local
     own_rows = pl.ds(pl.multiple_of(row_no * tile_rows, SUBLANES), tile_rows)
 
     own_fields = pltpu.make_async_copy(fields.at[row_no], state.at[:, own_rows], load_sem.at[0])
     own_depth = pltpu.make_async_copy(bathymetry, resting.at[own_rows], load_sem.at[1])
+    own_lists = pltpu.make_async_copy(lists_in, lists, load_sem.at[2])
     own_fields.start()
     own_depth.start()
+    own_lists.start()
 
     barrier = pltpu.get_barrier_semaphore()
 
@@ -172,132 +182,201 @@
             swaps.append(copy)
     own_fields.wait()
     own_depth.wait()
+    own_lists.wait()
     for copy in swaps:
         copy.wait()
 
-    depth[...] = resting[...].astype(jnp.float32) / 100.0
-    flux[...] = (depth[...] + state[0]) * state[1]
     lane = lax.broadcasted_iota(jnp.int32, (rows, LANES), 1)
-
-    def step(_, carry):
-        for col in range(cols):
-            advance(state, flux, depth, middle, flux_mid, None, time_step, col, rows, lane)
-        for col in range(cols):
-            advance(middle, flux_mid, depth, state, flux, state, 0.5 * time_step, col, rows, lane)
-        return carry
-
-    lax.fori_loop(0, STEPS * CYCLES, step, 0)
-
-    def piece(j, r):
-        return state.at[
+    steps = STEPS * CYCLES
+    share = -(-members // steps)
+
+    def compose(m):
+        source = m
+        for cycle_no in reversed(range(lists.shape[1])):
+            for section_no in reversed(range(lists.shape[0])):
+                source = lists[section_no, cycle_no, source]
+        sources[m] = source
+
+    def forecast(q):
+        first = q * chunk_cols
+        chunk = work.at[q]
+        for col in range(chunk_cols + 1):
+            here = pl.ds(col * LANES, LANES)
+            if col < chunk_cols:
+                source = pl.ds((first + col) * LANES, LANES)
+                tile = [state[kind, :, source] for kind in range(kinds)]
+                rest = resting[:, source]
+            else:
+                after = pl.ds((first + col) % cols * LANES, LANES)
+                before = pl.ds((first - 1) % cols * LANES, LANES)
+                follows = lane < LANES // 2
+                tile = [
+                    jnp.where(follows, state[kind, :, after], state[kind, :, before])
+                    for kind in range(kinds)
+                ]
+                rest = jnp.where(follows, resting[:, after], resting[:, before])
+            rest = rest.astype(jnp.float32) / 100.0
+            depth[:, here] = rest
+            for kind in range(kinds):
+                chunk[kind, :, here] = tile[kind]
+            flux[:, here] = (rest + tile[0]) * tile[1]
+
+        def step(i, carry):
+            if q == 0:
+                for n in range(share):
+                    compose(jnp.minimum(i * share + n, members - 1))
+            for col in range(chunk_cols + 1):
+                advance(chunk, flux, depth, middle, flux_mid, None, time_step, col, rows, lane)
+            for col in range(chunk_cols + 1):
+                advance(
+                    middle, flux_mid, depth, chunk, flux, chunk, 0.5 * time_step, col, rows, lane
+                )
+            return carry
+
+        lax.fori_loop(0, steps, step, 0)
+
+    seat = group // 2
+
+    def spread_copy(q, n, offset):
+        t = lax.rem(seat + offset, per_chunk)
+        j, r = 2 * t + lax.rem(t + q, 2), q // 2
+        src = work.at[
+            q,
             :,
-            pl.ds(pl.multiple_of(r * tile_rows + j // cols * part, SUBLANES), part),
-            pl.ds(pl.multiple_of(lax.rem(j, cols) * LANES, LANES), LANES),
+            pl.ds(pl.multiple_of(t // chunk_cols * SUBLANES, SUBLANES), SUBLANES),
+            pl.ds(pl.multiple_of(lax.rem(t, chunk_cols) * LANES, LANES), LANES),
         ]
-
-    def spread_copy(k):
-        other = lax.rem(me + k, devices)
-        j, r = other // rows_axis, lax.rem(other, rows_axis)
-        return pltpu.make_async_remote_copy(
-            src_ref=piece(j, r), dst_ref=held.at[me],
-            send_sem=spread_send.at[k], recv_sem=spread_recv,
+        remote = pltpu.make_async_remote_copy(
+            src_ref=src, dst_ref=held.at[me],
+            send_sem=spread_send.at[q, n], recv_sem=spread_recv,
             device_id=(j, r), device_id_type=MESH,
         )
-
-    def start_spread(k, carry):
-        spread_copy(k).start()
-        return carry
-
-    lax.fori_loop(1, devices, start_spread, 0)
-    pltpu.make_async_copy(piece(group, row_no), held.at[me], spread_recv).start()
-
-    def compose(m, carry):
-        source = m
-        for cycle_no in reversed(range(lists.shape[0])):
-            for section_no in reversed(range(lists.shape[1])):
-                source = lists[cycle_no, section_no, source]
-        sources[m] = source
-        return carry
-
-    lax.fori_loop(0, held.shape[0], compose, 0)
-    pltpu.make_async_copy(held, held, spread_recv).wait()
-
-    for m in range(held.shape[0]):
-        picked[m] = held[sources[m]]
-
+        return remote, src, j * rows_axis + r
+
+    def spread(q):
+        for n, offset in enumerate(alternate(per_chunk)):
+            remote, src, target = spread_copy(q, n, offset)
+            if offset:
+                remote.start()
+                continue
+
+            @pl.when(target != me)
+            def _():
+                remote.start()
+
+            @pl.when(target == me)
+            def _():
+                pltpu.make_async_copy(src, held.at[me], spread_recv).start()
+
+    my_chunk = 2 * row_no + lax.rem(group + seat, 2)
+    my_row = seat // chunk_cols * SUBLANES
+    home = my_row // tile_rows
     place = out.at[
         :,
         :,
-        pl.ds(pl.multiple_of(group // cols * part, SUBLANES), part),
-        pl.ds(pl.multiple_of(lax.rem(group, cols) * LANES, LANES), LANES),
+        pl.ds(pl.multiple_of(lax.rem(my_row, tile_rows), SUBLANES), SUBLANES),
+        pl.ds(
+            pl.multiple_of((my_chunk * chunk_cols + lax.rem(seat, chunk_cols)) * LANES, LANES),
+            LANES,
+        ),
     ]
 
-    def back_copy(k):
-        other = lax.rem(group + k, members_axis)
-        return pltpu.make_async_remote_copy(
-            src_ref=picked.at[pl.ds(other * local, local)], dst_ref=place,
-            send_sem=back_send.at[k], recv_sem=back_recv,
-            device_id=(other, row_no), device_id_type=MESH,
+    def back_copy(n, offset):
+        other = lax.rem(group + offset, members_axis)
+        src = picked.at[pl.ds(other * local, local)]
+        return src, pltpu.make_async_remote_copy(
+            src_ref=src, dst_ref=place,
+            send_sem=back_send.at[n], recv_sem=back_recv,
+            device_id=(other, home), device_id_type=MESH,
         )
 
-    def start_back(k, carry):
-        back_copy(k).start()
-        return carry
-
-    lax.fori_loop(1, members_axis, start_back, 0)
-    pltpu.make_async_copy(picked.at[pl.ds(group * local, local)], place, back_recv).start()
-
-    def end_spread(k, carry):
-        spread_copy(k).wait_send()
-        return carry
-
-    lax.fori_loop(1, devices, end_spread, 0)
-
-    def end_back(k, carry):
-        back_copy(k).wait_send()
-        return carry
-
-    lax.fori_loop(1, members_axis, end_back, 0)
+    def give_back():
+        pltpu.make_async_copy(held, held, spread_recv).wait()
+        for m in range(members):
+            picked[m] = held[sources[m]]
+        for n, offset in enumerate(alternate(members_axis)):
+            src, remote = back_copy(n, offset)
+            if offset:
+                remote.start()
+                continue
+
+            @pl.when(home != row_no)
+            def _():
+                remote.start()
+
+            @pl.when(home == row_no)
+            def _():
+                pltpu.make_async_copy(src, place, back_recv).start()
+
+    for q in range(chunks + LAG):
+        if q < chunks:
+            forecast(q)
+            spread(q)
+        if q >= LAG:
+
+            @pl.when(my_chunk == q - LAG)
+            def _():
+                give_back()
+
+    for q in range(chunks):
+        for n, offset in enumerate(alternate(per_chunk)):
+            remote, _, target = spread_copy(q, n, offset)
+            if offset:
+                remote.wait_send()
+                continue
+
+            @pl.when(target != me)
+            def _():
+                remote.wait_send()
+
+    for n, offset in enumerate(alternate(members_axis)):
+        _, remote = back_copy(n, offset)
+        if offset:
+            remote.wait_send()
+            continue
+
+        @pl.when(home != row_no)
+        def _():
+            remote.wait_send()
+
     pltpu.make_async_copy(out, out, back_recv).wait()
 
 
 def fast_body(members_axis, rows_axis, fields, bathymetry, copy_lists):
     local, kinds, tile_rows, width = fields.shape
     rows = tile_rows * rows_axis
-    part = tile_rows // (members_axis // (width // LANES))
+    chunks = 2 * rows_axis
+    chunk_width = width // chunks + LANES
+    members = members_axis * local
     f32 = jnp.float32
     dma = pltpu.SemaphoreType.DMA
     return pl.pallas_call(
         functools.partial(kernel, members_axis, rows_axis),
         out_shape=jax.ShapeDtypeStruct(fields.shape, f32),
-        in_specs=[
-            pl.BlockSpec(memory_space=pl.ANY),
-            pl.BlockSpec(memory_space=pl.ANY),
-            pl.BlockSpec(memory_space=pltpu.SMEM),
-        ],
-        out_specs=pl.BlockSpec(memory_space=pltpu.VMEM),
+        in_specs=[pl.BlockSpec(memory_space=pltpu.HBM)] * 3,
+        out_specs=pl.BlockSpec(memory_space=pltpu.HBM),
         scratch_shapes=[
             pltpu.VMEM((kinds, rows, width), f32),
-            pltpu.VMEM((kinds, rows, width), f32),
-            pltpu.VMEM((rows, width), f32),
-            pltpu.VMEM((rows, width), f32),
             pltpu.VMEM((rows, width), jnp.int32),
-            pltpu.VMEM((rows, width), f32),
-            pltpu.VMEM((members_axis * local, kinds, part, LANES), f32),
-            pltpu.VMEM((members_axis * local, kinds, part, LANES), f32),
-            pltpu.SMEM((members_axis * local,), jnp.int32),
-            dma((2,)),
+            pltpu.VMEM((chunks, kinds, rows, chunk_width), f32),
+            pltpu.VMEM((kinds, rows, chunk_width), f32),
+            pltpu.VMEM((rows, chunk_width), f32),
+            pltpu.VMEM((rows, chunk_width), f32),
+            pltpu.VMEM((rows, chunk_width), f32),
+            pltpu.VMEM((members, kinds, SUBLANES, LANES), f32),
+            pltpu.VMEM((members, kinds, SUBLANES, LANES), f32),
+            pltpu.SMEM((copy_lists.shape[1], copy_lists.shape[0], copy_lists.shape[2]), jnp.int32),
+            pltpu.SMEM((members,), jnp.int32),
+            dma((3,)),
             dma((2 * rows_axis,)),
             dma((2 * rows_axis,)),
-            dma((members_axis * rows_axis,)),
+            dma((chunks, members_axis // 2)),
             dma,
             dma((members_axis,)),
             dma,
         ],
-        compiler_params=pltpu.CompilerParams(
-            collective_id=0, has_side_effects=True, vmem_limit_bytes=32 * 1024 * 1024
-        ),
-    )(fields, bathymetry, copy_lists)
+        compiler_params=pltpu.CompilerParams(collective_id=0, has_side_effects=True),
+    )(fields, bathymetry, jnp.swapaxes(copy_lists, 0, 1))
 
 
 def solution(mesh):
@@ -306,13 +385,15 @@
 
     def body(fields, bathymetry, copy_lists):
         local, _, tile_rows, width = fields.shape
-        cols = width // LANES
-        splits = max(members_axis // cols, 1)
+        chunks = 2 * rows_axis
+        chunk_cols = width // (LANES * chunks)
+        row_tiles = tile_rows * rows_axis // SUBLANES
         fits = (
             local == rows_axis
-            and width % LANES == 0
-            and members_axis % cols == 0
-            and tile_rows % (splits * SUBLANES) == 0
+            and width % (LANES * chunks) == 0
+            and tile_rows % SUBLANES == 0
+            and members_axis == 2 * row_tiles * chunk_cols
+            and 2 * STEPS * CYCLES <= LANES // 2
         )
         if fits:
             return fast_body(members_axis, rows_axis, fields, bathymetry, copy_lists)

time: 37.1 us -> 40.8 us (1.100)
  the two profiles are of different devices: /device:TPU:28 before, /device:TPU:1 now
where the time goes in v4:
time: 40.8 us; the launch traced here: 40.6 us
  Pallas kernels  38.8 us (95%)
  local copies, waits for them, and re-layouts  1.77 us (4%)
    pallas_call x1, Pallas kernels, fast_body(): pl.pallas_call(functools.partial(kernel, members_axis, rows_axis), out_sh...  38.8 us
    unnamed x1, local copies, waits for them, and re-layouts  1.77 us

profile of v4, /device:TPU:1, one launch (start us, length us, event | category | flops | bytes accessed | tf_op | source)
XLA Modules:
  0.0 40.6 jit_solution(10591628882356603435)
XLA Ops:
  0.0 38.8 %shard_map.37 = f32[2,3,16,1024]{3,2,1,0:T(8,128)} custom-call(f32[2,3,16,1024]{3,2,1,0:T(8,128)} %fields.1, s32[16,1024]{1,0:T(8,128)} %bathymetry.1, s32[5,3,32]{2,1,0:T(4,128)} %bitcast.1), custom_call_target="tpu_custom_call" | custom-call | tf_op jit(solution)/shard_map/pallas_call | solution.py:353
  38.8 1.8 %copy.5 = f32[2,3,16,1024]{3,2,1,0:T(8,128)} copy(f32[2,3,16,1024]{3,2,1,0:T(8,128)} %shard_map.37) | data formatting | bytes 786432

commit v5 on v3

--- a/solution.py
+++ b/solution.py
@@ -86,47 +86,52 @@
     )
 
 
-def advance(state, flux, depth, target, target_flux, base, scale, col, rows, lane):
-    cols = state.shape[2] // LANES
+def advance(state, flux, depth, target, target_flux, base, scale, col, lane):
+    cols = state.shape[-1] // LANES
+    count = state.shape[1]
     here = pl.ds(col * LANES, LANES)
     left = pl.ds((col - 1) % cols * LANES, LANES)
     right = pl.ds((col + 1) % cols * LANES, LANES)
-
-    def from_left(ref):
-        return pltpu.roll(jnp.where(lane == LANES - 1, ref[:, left], ref[:, here]), 1, 1)
-
-    def from_right(ref):
-        return pltpu.roll(jnp.where(lane == 0, ref[:, right], ref[:, here]), LANES - 1, 1)
-
-    height = state[0, :, here]
-    east = state[1, :, here]
-    north = state[2, :, here]
-    rest = depth[:, here]
-    flux_y = (rest + height) * north
-    diff_x = from_right(flux) - from_left(flux)
-    diff_y = pltpu.roll(flux_y, rows - 1, 0) - pltpu.roll(flux_y, 1, 0)
-    slope_x = from_right(state.at[0]) - from_left(state.at[0])
-    slope_y = pltpu.roll(height, rows - 1, 0) - pltpu.roll(height, 1, 0)
+    first_lane, last_lane = lane == 0, lane == LANES - 1
+
+    def slope_east(ref, k):
+        own = ref[k, :, here]
+        after = pltpu.roll(jnp.where(first_lane, ref[k, :, right], own), LANES - 1, 1)
+        before = pltpu.roll(jnp.where(last_lane, ref[k, :, left], own), 1, 1)
+        return after - before
+
+    def slope_north(tiles, k):
+        after = tiles[k + 1] if k + 1 < count else pltpu.roll(tiles[0], SUBLANES - 1, 0)
+        before = tiles[k - 1] if k > 0 else pltpu.roll(tiles[count - 1], 1, 0)
+        return after - before
+
     keep = 1.0 if base is None else 0.5
     drag = keep - scale * friction
     turn = scale * coriolis
     push = 0.5 * gravity * scale
-    new_h = (height if base is None else 0.5 * height) - (0.5 * scale) * (diff_x + diff_y)
-    new_u = drag * east + turn * north - push * slope_x
-    new_v = drag * north - turn * east - push * slope_y
-    if base is not None:
-        new_h = new_h + 0.5 * base[0, :, here]
-        new_u = new_u + 0.5 * base[1, :, here]
-        new_v = new_v + 0.5 * base[2, :, here]
-    target[0, :, here] = new_h
-    target[1, :, here] = new_u
-    target[2, :, here] = new_v
-    target_flux[:, here] = (rest + new_h) * new_u
+    heights = [state[0, k, :, here] for k in range(count)]
+    norths = [state[2, k, :, here] for k in range(count)]
+    rests = [depth[k, :, here] for k in range(count)]
+    fluxes = [(rests[k] + heights[k]) * norths[k] for k in range(count)]
+    for k in range(count):
+        height, north, east = heights[k], norths[k], state[1, k, :, here]
+        spread_out = slope_east(flux, k) + slope_north(fluxes, k)
+        new_h = (height if base is None else 0.5 * height) - (0.5 * scale) * spread_out
+        new_u = drag * east + turn * north - push * slope_east(state.at[0], k)
+        new_v = drag * north - turn * east - push * slope_north(heights, k)
+        if base is not None:
+            new_h = new_h + 0.5 * base[0, k, :, here]
+            new_u = new_u + 0.5 * base[1, k, :, here]
+            new_v = new_v + 0.5 * base[2, k, :, here]
+        target[0, k, :, here] = new_h
+        target[1, k, :, here] = new_u
+        target[2, k, :, here] = new_v
+        target_flux[k, :, here] = (rests[k] + new_h) * new_u
 
 
 def kernel(
     members_axis, rows_axis, fields, bathymetry, lists_in, out,
-    state, middle, flux, flux_mid, resting, depth, held, picked, lists, sources,
+    state, stage, dealt, middle, flux, flux_mid, resting, depth, held, picked, lists, sources,
     load_sem, swap_send, swap_recv, spread_send, spread_recv, back_send, back_recv,
 ):
     group, row_no = lax.axis_index("member"), lax.axis_index("row")
@@ -177,24 +182,42 @@
     for copy in swaps:
         copy.wait()
 
-    depth[...] = resting[...].astype(jnp.float32) / 100.0
-    flux[...] = (depth[...] + state[0]) * state[1]
-    lane = lax.broadcasted_iota(jnp.int32, (rows, LANES), 1)
+    count = dealt.shape[1]
+    lane = lax.broadcasted_iota(jnp.int32, (SUBLANES, LANES), 1)
+    for col in range(cols):
+        here = pl.ds(col * LANES, LANES)
+        for kind in range(3):
+            stage[kind, col] = state[kind, :, here]
+        stage[3, col] = resting[:, here].astype(jnp.float32) / 100.0
+        for k in range(count):
+            every = pl.ds(k, SUBLANES, stride=count)
+            height, east = stage[0, col, every], stage[1, col, every]
+            rest = stage[3, col, every]
+            dealt[0, k, :, here] = height
+            dealt[1, k, :, here] = east
+            dealt[2, k, :, here] = stage[2, col, every]
+            depth[k, :, here] = rest
+            flux[k, :, here] = (rest + height) * east
 
     def step(_, carry):
         for col in range(cols):
-            advance(state, flux, depth, middle, flux_mid, None, time_step, col, rows, lane)
+            advance(dealt, flux, depth, middle, flux_mid, None, time_step, col, lane)
         for col in range(cols):
-            advance(middle, flux_mid, depth, state, flux, state, 0.5 * time_step, col, rows, lane)
+            advance(middle, flux_mid, depth, dealt, flux, dealt, 0.5 * time_step, col, lane)
         return carry
 
     lax.fori_loop(0, STEPS * CYCLES, step, 0)
+    for col in range(cols):
+        here = pl.ds(col * LANES, LANES)
+        for k in range(count):
+            for kind in range(3):
+                stage[kind, col, pl.ds(k, SUBLANES, stride=count)] = dealt[kind, k, :, here]
 
     def piece(kind, j, r):
-        return state.at[
+        return stage.at[
             kind,
+            lax.rem(j, cols),
             pl.ds(pl.multiple_of(r * tile_rows + j // cols * part, SUBLANES), part),
-            pl.ds(pl.multiple_of(lax.rem(j, cols) * LANES, LANES), LANES),
         ]
 
     def spread_copy(kind, other):
@@ -292,6 +315,7 @@
 def fast_body(members_axis, rows_axis, fields, bathymetry, copy_lists):
     local, kinds, tile_rows, width = fields.shape
     rows = tile_rows * rows_axis
+    count = rows // SUBLANES
     part = tile_rows // (members_axis // (width // LANES))
     f32 = jnp.float32
     dma = pltpu.SemaphoreType.DMA
@@ -306,11 +330,13 @@
         out_specs=pl.BlockSpec(memory_space=pltpu.VMEM),
         scratch_shapes=[
             pltpu.VMEM((kinds, rows, width), f32),
-            pltpu.VMEM((kinds, rows, width), f32),
-            pltpu.VMEM((rows, width), f32),
-            pltpu.VMEM((rows, width), f32),
+            pltpu.VMEM((kinds + 1, width // LANES, rows, LANES), f32),
+            pltpu.VMEM((kinds, count, SUBLANES, width), f32),
+            pltpu.VMEM((kinds, count, SUBLANES, width), f32),
+            pltpu.VMEM((count, SUBLANES, width), f32),
+            pltpu.VMEM((count, SUBLANES, width), f32),
             pltpu.VMEM((rows, width), jnp.int32),
-            pltpu.VMEM((rows, width), f32),
+            pltpu.VMEM((count, SUBLANES, width), f32),
             [pltpu.VMEM((members_axis * local, part, LANES), f32)] * kinds,
             [pltpu.VMEM((members_axis * local, part, LANES), f32)] * kinds,
             pltpu.SMEM((copy_lists.shape[1], copy_lists.shape[0], copy_lists.shape[2]), jnp.int32),

time: 36.5 us -> 36.3 us (level)
  no operation moved by 1% of the time
where the time goes in v5:
time: 36.3 us; the launch traced here: 36.2 us
  Pallas kernels  34.4 us (95%)
  local copies, waits for them, and re-layouts  1.77 us (5%)
    pallas_call x1, Pallas kernels, fast_body(): pl.pallas_call(functools.partial(kernel, members_axis, rows_axis), out_sh...  34.4 us
    unnamed x1, local copies, waits for them, and re-layouts  1.77 us

profile of v5, /device:TPU:0, one launch (start us, length us, event | category | flops | bytes accessed | tf_op | source)
XLA Modules:
  0.0 36.2 jit_solution(18295976741626549630)
XLA Ops:
  0.0 34.4 %shard_map.37 = f32[2,3,16,1024]{3,2,1,0:T(8,128)} custom-call(f32[2,3,16,1024]{3,2,1,0:T(8,128)} %fields.1, s32[16,1024]{1,0:T(8,128)} %bathymetry.1, s32[5,3,32]{2,1,0:T(4,128)} %bitcast.1), custom_call_target="tpu_custom_call" | custom-call | tf_op jit(solution)/shard_map/pallas_call | solution.py:322
  34.4 1.8 %copy.5 = f32[2,3,16,1024]{3,2,1,0:T(8,128)} copy(f32[2,3,16,1024]{3,2,1,0:T(8,128)} %shard_map.37) | data formatting | bytes 786432

commit v6 on v5

--- a/solution.py
+++ b/solution.py
@@ -131,7 +131,8 @@
 
 def kernel(
     members_axis, rows_axis, fields, bathymetry, lists_in, out,
-    state, stage, dealt, middle, flux, flux_mid, resting, depth, held, picked, lists, sources,
+    state, stage, dealt, middle, flux, flux_mid, resting, depth, packed, held, picked, landed,
+    lists, sources,
     load_sem, swap_send, swap_recv, spread_send, spread_recv, back_send, back_recv,
 ):
     group, row_no = lax.axis_index("member"), lax.axis_index("row")
@@ -141,7 +142,6 @@
     rows = tile_rows * rows_axis
     cols = width // LANES
     local = fields.shape[0]
-    part = held[0].shape[1]
     own_rows = pl.ds(pl.multiple_of(row_no * tile_rows, SUBLANES), tile_rows)
 
     own_fields = pltpu.make_async_copy(fields.at[row_no], state.at[:, own_rows], load_sem.at[0])
@@ -212,40 +212,35 @@
         for k in range(count):
             for kind in range(3):
                 stage[kind, col, pl.ds(k, SUBLANES, stride=count)] = dealt[kind, k, :, here]
-
-    def piece(kind, j, r):
-        return stage.at[
-            kind,
-            lax.rem(j, cols),
-            pl.ds(pl.multiple_of(r * tile_rows + j // cols * part, SUBLANES), part),
-        ]
-
-    def spread_copy(kind, other):
+        for k in range(count):
+            for kind in range(3):
+                packed[col, k, kind] = stage[kind, col, pl.ds(k * SUBLANES, SUBLANES)]
+
+    def piece(j, r):
+        return packed.at[lax.rem(j, cols), r * (tile_rows // SUBLANES) + j // cols]
+
+    def spread_copy(other):
         j, r = other // rows_axis, lax.rem(other, rows_axis)
         return pltpu.make_async_remote_copy(
-            src_ref=piece(kind, j, r), dst_ref=held[kind].at[me],
-            send_sem=spread_send.at[kind, other], recv_sem=spread_recv.at[kind],
+            src_ref=piece(j, r), dst_ref=held.at[me],
+            send_sem=spread_send.at[other], recv_sem=spread_recv,
             device_id=(j, r), device_id_type=MESH,
         )
 
     half = devices // 2
     side, seat = me // half, lax.rem(me, half)
     far, near = (1 - side) * half, side * half
-    kinds = state.shape[0]
-
-    for kind in range(kinds):
-        spread_copy(kind, far + seat).start()
-
-        def start_spread(k, carry, kind=kind):
-            there = lax.rem(seat + k, half)
-            spread_copy(kind, far + there).start()
-            spread_copy(kind, near + there).start()
-            return carry
-
-        lax.fori_loop(1, half, start_spread, 0)
-        pltpu.make_async_copy(
-            piece(kind, group, row_no), held[kind].at[me], spread_recv.at[kind]
-        ).start()
+
+    spread_copy(far + seat).start()
+
+    def start_spread(k, carry):
+        there = lax.rem(seat + k, half)
+        spread_copy(far + there).start()
+        spread_copy(near + there).start()
+        return carry
+
+    lax.fori_loop(1, half, start_spread, 0)
+    pltpu.make_async_copy(piece(group, row_no), held.at[me], spread_recv).start()
 
     own_lists.wait()
 
@@ -259,18 +254,10 @@
 
     lax.fori_loop(0, sources.shape[0], compose, 0)
 
-    def place(kind):
-        return out.at[
-            :,
-            kind,
-            pl.ds(pl.multiple_of(group // cols * part, SUBLANES), part),
-            pl.ds(pl.multiple_of(lax.rem(group, cols) * LANES, LANES), LANES),
-        ]
-
-    def back_copy(kind, other):
+    def back_copy(other):
         return pltpu.make_async_remote_copy(
-            src_ref=picked[kind].at[pl.ds(other * local, local)], dst_ref=place(kind),
-            send_sem=back_send.at[kind, other], recv_sem=back_recv.at[kind],
+            src_ref=picked.at[other], dst_ref=landed.at[group],
+            send_sem=back_send.at[other], recv_sem=back_recv,
             device_id=(other, row_no), device_id_type=MESH,
         )
 
@@ -278,45 +265,43 @@
     back_side, back_seat = group // back_half, lax.rem(group, back_half)
     back_far, back_near = (1 - back_side) * back_half, back_side * back_half
 
-    for kind in range(kinds):
-        pltpu.make_async_copy(held[kind], held[kind], spread_recv.at[kind]).wait()
-        for m in range(sources.shape[0]):
-            picked[kind][m] = held[kind][sources[m]]
-        back_copy(kind, back_far + back_seat).start()
-
-        def start_back(k, carry, kind=kind):
-            there = lax.rem(back_seat + k, back_half)
-            back_copy(kind, back_far + there).start()
-            back_copy(kind, back_near + there).start()
-            return carry
-
-        lax.fori_loop(1, back_half, start_back, 0)
-        pltpu.make_async_copy(
-            picked[kind].at[pl.ds(group * local, local)], place(kind), back_recv.at[kind]
-        ).start()
-
-    for kind in range(kinds):
-
-        def end_spread(k, carry, kind=kind):
-            spread_copy(kind, lax.rem(me + k, devices)).wait_send()
-            return carry
-
-        lax.fori_loop(1, devices, end_spread, 0)
-
-        def end_back(k, carry, kind=kind):
-            back_copy(kind, lax.rem(group + k, members_axis)).wait_send()
-            return carry
-
-        lax.fori_loop(1, members_axis, end_back, 0)
-    for kind in range(kinds):
-        pltpu.make_async_copy(out.at[:, kind], out.at[:, kind], back_recv.at[kind]).wait()
+    pltpu.make_async_copy(held, held, spread_recv).wait()
+    for m in range(sources.shape[0]):
+        picked[m // local, m % local] = held[sources[m]]
+    back_copy(back_far + back_seat).start()
+
+    def start_back(k, carry):
+        there = lax.rem(back_seat + k, back_half)
+        back_copy(back_far + there).start()
+        back_copy(back_near + there).start()
+        return carry
+
+    lax.fori_loop(1, back_half, start_back, 0)
+    pltpu.make_async_copy(picked.at[group], landed.at[group], back_recv).start()
+
+    def end_spread(k, carry):
+        spread_copy(lax.rem(me + k, devices)).wait_send()
+        return carry
+
+    lax.fori_loop(1, devices, end_spread, 0)
+
+    def end_back(k, carry):
+        back_copy(lax.rem(group + k, members_axis)).wait_send()
+        return carry
+
+    lax.fori_loop(1, members_axis, end_back, 0)
+    pltpu.make_async_copy(landed, landed, back_recv).wait()
+    for j in range(members_axis):
+        tile = pl.ds(j // cols * SUBLANES, SUBLANES), pl.ds(j % cols * LANES, LANES)
+        for m in range(local):
+            for kind in range(3):
+                out[m, kind, tile[0], tile[1]] = landed[j, m, kind]
 
 
 def fast_body(members_axis, rows_axis, fields, bathymetry, copy_lists):
     local, kinds, tile_rows, width = fields.shape
     rows = tile_rows * rows_axis
     count = rows // SUBLANES
-    part = tile_rows // (members_axis // (width // LANES))
     f32 = jnp.float32
     dma = pltpu.SemaphoreType.DMA
     return pl.pallas_call(
@@ -337,17 +322,19 @@
             pltpu.VMEM((count, SUBLANES, width), f32),
             pltpu.VMEM((rows, width), jnp.int32),
             pltpu.VMEM((count, SUBLANES, width), f32),
-            [pltpu.VMEM((members_axis * local, part, LANES), f32)] * kinds,
-            [pltpu.VMEM((members_axis * local, part, LANES), f32)] * kinds,
+            pltpu.VMEM((width // LANES, count, kinds, SUBLANES, LANES), f32),
+            pltpu.VMEM((members_axis * local, kinds, SUBLANES, LANES), f32),
+            pltpu.VMEM((members_axis, local, kinds, SUBLANES, LANES), f32),
+            pltpu.VMEM((members_axis, local, kinds, SUBLANES, LANES), f32),
             pltpu.SMEM((copy_lists.shape[1], copy_lists.shape[0], copy_lists.shape[2]), jnp.int32),
             pltpu.SMEM((members_axis * local,), jnp.int32),
             dma((3,)),
             dma((2 * rows_axis,)),
             dma((2 * rows_axis,)),
-            dma((kinds, members_axis * rows_axis)),
-            dma((kinds,)),
-            dma((kinds, members_axis)),
-            dma((kinds,)),
+            dma((members_axis * rows_axis,)),
+            dma,
+            dma((members_axis,)),
+            dma,
         ],
         compiler_params=pltpu.CompilerParams(
             collective_id=0, has_side_effects=True
@@ -368,7 +355,7 @@
             and width % LANES == 0
             and members_axis % cols == 0
             and members_axis % 2 == 0
-            and tile_rows % (splits * SUBLANES) == 0
+            and tile_rows == splits * SUBLANES
         )
         if fits:
             return fast_body(members_axis, rows_axis, fields, bathymetry, copy_lists)

time: 36.3 us -> 38.1 us (1.050)
  Pallas kernels: 34.4 us -> 36.2 us
    pallas_call x1, Pallas kernels: 34.4 us -> 36.2 us  [fast_body(): pl.pallas_call(functools.partial(kernel, members_axis, rows_axis), out_sh...]
where the time goes in v6:
time: 38.1 us; the launch traced here: 38 us
  Pallas kernels  36.2 us (95%)
  local copies, waits for them, and re-layouts  1.77 us (5%)
    pallas_call x1, Pallas kernels, fast_body(): pl.pallas_call(functools.partial(kernel, members_axis, rows_axis), out_sh...  36.2 us
    unnamed x1, local copies, waits for them, and re-layouts  1.77 us

profile of v6, /device:TPU:0, one launch (start us, length us, event | category | flops | bytes accessed | tf_op | source)
XLA Modules:
  0.0 38.0 jit_solution(2054391300255718634)
XLA Ops:
  0.0 36.2 %shard_map.37 = f32[2,3,16,1024]{3,2,1,0:T(8,128)} custom-call(f32[2,3,16,1024]{3,2,1,0:T(8,128)} %fields.1, s32[16,1024]{1,0:T(8,128)} %bathymetry.1, s32[5,3,32]{2,1,0:T(4,128)} %bitcast.1), custom_call_target="tpu_custom_call" | custom-call | tf_op jit(solution)/shard_map/pallas_call | solution.py:307
  36.2 1.8 %copy.5 = f32[2,3,16,1024]{3,2,1,0:T(8,128)} copy(f32[2,3,16,1024]{3,2,1,0:T(8,128)} %shard_map.37) | data formatting | bytes 786432

commit v7 on v6

--- a/solution.py
+++ b/solution.py
@@ -19,6 +19,7 @@
 LANES = 128
 SUBLANES = 8
 MESH = pl.DeviceIdType.MESH
+CHUNKS = 2
 
 
 def extended(x, sides, width):
@@ -131,7 +132,7 @@
 
 def kernel(
     members_axis, rows_axis, fields, bathymetry, lists_in, out,
-    state, stage, dealt, middle, flux, flux_mid, resting, depth, packed, held, picked, landed,
+    state, stage, dealt, deep, work, middle, flux, flux_mid, resting, depth, sent, held, picked,
     lists, sources,
     load_sem, swap_send, swap_recv, spread_send, spread_recv, back_send, back_recv,
 ):
@@ -191,117 +192,176 @@
         stage[3, col] = resting[:, here].astype(jnp.float32) / 100.0
         for k in range(count):
             every = pl.ds(k, SUBLANES, stride=count)
-            height, east = stage[0, col, every], stage[1, col, every]
-            rest = stage[3, col, every]
-            dealt[0, k, :, here] = height
-            dealt[1, k, :, here] = east
-            dealt[2, k, :, here] = stage[2, col, every]
-            depth[k, :, here] = rest
-            flux[k, :, here] = (rest + height) * east
-
-    def step(_, carry):
-        for col in range(cols):
-            advance(dealt, flux, depth, middle, flux_mid, None, time_step, col, lane)
-        for col in range(cols):
-            advance(middle, flux_mid, depth, dealt, flux, dealt, 0.5 * time_step, col, lane)
-        return carry
-
-    lax.fori_loop(0, STEPS * CYCLES, step, 0)
-    for col in range(cols):
-        here = pl.ds(col * LANES, LANES)
-        for k in range(count):
             for kind in range(3):
-                stage[kind, col, pl.ds(k, SUBLANES, stride=count)] = dealt[kind, k, :, here]
-        for k in range(count):
-            for kind in range(3):
-                packed[col, k, kind] = stage[kind, col, pl.ds(k * SUBLANES, SUBLANES)]
-
-    def piece(j, r):
-        return packed.at[lax.rem(j, cols), r * (tile_rows // SUBLANES) + j // cols]
-
-    def spread_copy(other):
-        j, r = other // rows_axis, lax.rem(other, rows_axis)
-        return pltpu.make_async_remote_copy(
-            src_ref=piece(j, r), dst_ref=held.at[me],
-            send_sem=spread_send.at[other], recv_sem=spread_recv,
-            device_id=(j, r), device_id_type=MESH,
-        )
-
-    half = devices // 2
-    side, seat = me // half, lax.rem(me, half)
-    far, near = (1 - side) * half, side * half
-
-    spread_copy(far + seat).start()
-
-    def start_spread(k, carry):
-        there = lax.rem(seat + k, half)
-        spread_copy(far + there).start()
-        spread_copy(near + there).start()
-        return carry
-
-    lax.fori_loop(1, half, start_spread, 0)
-    pltpu.make_async_copy(piece(group, row_no), held.at[me], spread_recv).start()
+                dealt[kind, k, :, here] = stage[kind, col, every]
+            deep[k, :, here] = stage[3, col, every]
 
     own_lists.wait()
-
-    def compose(m, carry):
+    steps = STEPS * CYCLES
+    members = sources.shape[0]
+    share = -(-members // steps)
+
+    def compose(m):
         source = m
         for cycle_no in reversed(range(lists.shape[1])):
             for section_no in reversed(range(lists.shape[0])):
                 source = lists[section_no, cycle_no, source]
         sources[m] = source
-        return carry
-
-    lax.fori_loop(0, sources.shape[0], compose, 0)
-
-    def back_copy(other):
-        return pltpu.make_async_remote_copy(
-            src_ref=picked.at[other], dst_ref=landed.at[group],
-            send_sem=back_send.at[other], recv_sem=back_recv,
-            device_id=(other, row_no), device_id_type=MESH,
+
+    chunk_cols = cols // CHUNKS
+
+    def forecast(q):
+        first = q * chunk_cols
+        follows = lane < LANES // 2
+        for col in range(chunk_cols + 1):
+            here = pl.ds(col * LANES, LANES)
+            after = pl.ds((first + col) % cols * LANES, LANES)
+            before = pl.ds((first - 1) % cols * LANES, LANES)
+
+            def taken(ref, k, col=col, after=after, before=before):
+                if col < chunk_cols:
+                    return ref[k, :, after]
+                return jnp.where(follows, ref[k, :, after], ref[k, :, before])
+
+            for k in range(count):
+                height, east, north = [taken(dealt.at[kind], k) for kind in range(3)]
+                rest = taken(deep, k)
+                work[0, k, :, here] = height
+                work[1, k, :, here] = east
+                work[2, k, :, here] = north
+                depth[k, :, here] = rest
+                flux[k, :, here] = (rest + height) * east
+
+        def step(i, carry):
+            if q == 0:
+                for n in range(share):
+                    compose(jnp.minimum(i * share + n, members - 1))
+            for col in range(chunk_cols + 1):
+                advance(work, flux, depth, middle, flux_mid, None, time_step, col, lane)
+            for col in range(chunk_cols + 1):
+                advance(middle, flux_mid, depth, work, flux, work, 0.5 * time_step, col, lane)
+            return carry
+
+        lax.fori_loop(0, steps, step, 0)
+        for col in range(chunk_cols):
+            here = pl.ds(col * LANES, LANES)
+            for k in range(count):
+                for kind in range(3):
+                    sent[q][kind, col, pl.ds(k, SUBLANES, stride=count)] = work[kind, k, :, here]
+
+    stages = [(q, kind) for q in range(CHUNKS) for kind in range(3)]
+
+    def core_of(i):
+        return sum(stages[i]) % rows_axis
+
+    def spread_copy(i, j):
+        q, kind = stages[i]
+        src = sent[q].at[
+            kind,
+            lax.rem(j, chunk_cols),
+            pl.ds(pl.multiple_of(j // chunk_cols * SUBLANES, SUBLANES), SUBLANES),
+        ]
+        return src, pltpu.make_async_remote_copy(
+            src_ref=src, dst_ref=held[i].at[me],
+            send_sem=spread_send.at[i, j], recv_sem=spread_recv.at[i],
+            device_id=(j, core_of(i)), device_id_type=MESH,
         )
 
-    back_half = members_axis // 2
-    back_side, back_seat = group // back_half, lax.rem(group, back_half)
-    back_far, back_near = (1 - back_side) * back_half, back_side * back_half
-
-    pltpu.make_async_copy(held, held, spread_recv).wait()
-    for m in range(sources.shape[0]):
-        picked[m // local, m % local] = held[sources[m]]
-    back_copy(back_far + back_seat).start()
-
-    def start_back(k, carry):
-        there = lax.rem(back_seat + k, back_half)
-        back_copy(back_far + there).start()
-        back_copy(back_near + there).start()
-        return carry
-
-    lax.fori_loop(1, back_half, start_back, 0)
-    pltpu.make_async_copy(picked.at[group], landed.at[group], back_recv).start()
-
-    def end_spread(k, carry):
-        spread_copy(lax.rem(me + k, devices)).wait_send()
-        return carry
-
-    lax.fori_loop(1, devices, end_spread, 0)
-
-    def end_back(k, carry):
-        back_copy(lax.rem(group + k, members_axis)).wait_send()
-        return carry
-
-    lax.fori_loop(1, members_axis, end_back, 0)
-    pltpu.make_async_copy(landed, landed, back_recv).wait()
-    for j in range(members_axis):
-        tile = pl.ds(j // cols * SUBLANES, SUBLANES), pl.ds(j % cols * LANES, LANES)
-        for m in range(local):
-            for kind in range(3):
-                out[m, kind, tile[0], tile[1]] = landed[j, m, kind]
+    half = members_axis // 2
+    side, seat = group // half, lax.rem(group, half)
+    far, near = (1 - side) * half, side * half
+
+    def send_all(copy, own_is_local, own_dst, own_sem):
+        copy(far + seat)[1].start()
+
+        def start(k, carry):
+            there = lax.rem(seat + k, half)
+            copy(far + there)[1].start()
+            copy(near + there)[1].start()
+            return carry
+
+        lax.fori_loop(1, half, start, 0)
+        src, remote = copy(group)
+
+        @pl.when(own_is_local)
+        def _():
+            pltpu.make_async_copy(src, own_dst, own_sem).start()
+
+        @pl.when(jnp.logical_not(own_is_local))
+        def _():
+            remote.start()
+
+    def end_all(copy, own_is_local):
+        def end(k, carry):
+            copy(lax.rem(group + k, members_axis))[1].wait_send()
+            return carry
+
+        lax.fori_loop(1, members_axis, end, 0)
+
+        @pl.when(jnp.logical_not(own_is_local))
+        def _():
+            copy(group)[1].wait_send()
+
+    my_row = group // chunk_cols * SUBLANES
+    home = my_row // tile_rows
+
+    def place(i):
+        q, kind = stages[i]
+        return out.at[
+            :,
+            kind,
+            pl.ds(pl.multiple_of(lax.rem(my_row, tile_rows), SUBLANES), SUBLANES),
+            pl.ds(
+                pl.multiple_of((q * chunk_cols + lax.rem(group, chunk_cols)) * LANES, LANES),
+                LANES,
+            ),
+        ]
+
+    def back_copy(i, other):
+        src = picked[i].at[pl.ds(other * local, local)]
+        return src, pltpu.make_async_remote_copy(
+            src_ref=src, dst_ref=place(i),
+            send_sem=back_send.at[i, other], recv_sem=back_recv.at[i],
+            device_id=(other, home), device_id_type=MESH,
+        )
+
+    for q in range(CHUNKS):
+        forecast(q)
+        for i in range(3 * q, 3 * q + 3):
+            send_all(
+                functools.partial(spread_copy, i),
+                row_no == core_of(i), held[i].at[me], spread_recv.at[i],
+            )
+
+    for i in range(len(stages)):
+
+        @pl.when(row_no == core_of(i))
+        def _(i=i):
+            pltpu.make_async_copy(held[i], held[i], spread_recv.at[i]).wait()
+            for m in range(members):
+                picked[i][m] = held[i][sources[m]]
+            send_all(
+                functools.partial(back_copy, i), row_no == home, place(i), back_recv.at[i]
+            )
+
+    for i, (q, kind) in enumerate(stages):
+        end_all(functools.partial(spread_copy, i), row_no == core_of(i))
+
+        @pl.when(row_no == core_of(i))
+        def _(i=i):
+            end_all(functools.partial(back_copy, i), row_no == home)
+
+    for i, (q, kind) in enumerate(stages):
+        landed = out.at[:, kind, :, pl.ds(q * chunk_cols * LANES, chunk_cols * LANES)]
+        pltpu.make_async_copy(landed, landed, back_recv.at[i]).wait()
 
 
 def fast_body(members_axis, rows_axis, fields, bathymetry, copy_lists):
     local, kinds, tile_rows, width = fields.shape
     rows = tile_rows * rows_axis
     count = rows // SUBLANES
+    chunk_width = width // CHUNKS + LANES
+    members = members_axis * local
     f32 = jnp.float32
     dma = pltpu.SemaphoreType.DMA
     return pl.pallas_call(
@@ -317,24 +377,25 @@
             pltpu.VMEM((kinds, rows, width), f32),
             pltpu.VMEM((kinds + 1, width // LANES, rows, LANES), f32),
             pltpu.VMEM((kinds, count, SUBLANES, width), f32),
-            pltpu.VMEM((kinds, count, SUBLANES, width), f32),
             pltpu.VMEM((count, SUBLANES, width), f32),
-            pltpu.VMEM((count, SUBLANES, width), f32),
+            pltpu.VMEM((kinds, count, SUBLANES, chunk_width), f32),
+            pltpu.VMEM((kinds, count, SUBLANES, chunk_width), f32),
+            pltpu.VMEM((count, SUBLANES, chunk_width), f32),
+            pltpu.VMEM((count, SUBLANES, chunk_width), f32),
             pltpu.VMEM((rows, width), jnp.int32),
-            pltpu.VMEM((count, SUBLANES, width), f32),
-            pltpu.VMEM((width // LANES, count, kinds, SUBLANES, LANES), f32),
-            pltpu.VMEM((members_axis * local, kinds, SUBLANES, LANES), f32),
-            pltpu.VMEM((members_axis, local, kinds, SUBLANES, LANES), f32),
-            pltpu.VMEM((members_axis, local, kinds, SUBLANES, LANES), f32),
+            pltpu.VMEM((count, SUBLANES, chunk_width), f32),
+            [pltpu.VMEM((kinds, width // LANES // CHUNKS, rows, LANES), f32)] * CHUNKS,
+            [pltpu.VMEM((members, SUBLANES, LANES), f32)] * (CHUNKS * kinds),
+            [pltpu.VMEM((members, SUBLANES, LANES), f32)] * (CHUNKS * kinds),
             pltpu.SMEM((copy_lists.shape[1], copy_lists.shape[0], copy_lists.shape[2]), jnp.int32),
-            pltpu.SMEM((members_axis * local,), jnp.int32),
+            pltpu.SMEM((members,), jnp.int32),
             dma((3,)),
             dma((2 * rows_axis,)),
             dma((2 * rows_axis,)),
-            dma((members_axis * rows_axis,)),
-            dma,
-            dma((members_axis,)),
-            dma,
+            dma((CHUNKS * kinds, members_axis)),
+            dma((CHUNKS * kinds,)),
+            dma((CHUNKS * kinds, members_axis)),
+            dma((CHUNKS * kinds,)),
         ],
         compiler_params=pltpu.CompilerParams(
             collective_id=0, has_side_effects=True
@@ -348,14 +409,15 @@
 
     def body(fields, bathymetry, copy_lists):
         local, _, tile_rows, width = fields.shape
-        cols = width // LANES
-        splits = max(members_axis // cols, 1)
+        chunk_cols = width // (LANES * CHUNKS)
+        row_tiles = tile_rows * rows_axis // SUBLANES
         fits = (
             local == rows_axis
-            and width % LANES == 0
-            and members_axis % cols == 0
+            and width % (LANES * CHUNKS) == 0
+            and tile_rows % SUBLANES == 0
             and members_axis % 2 == 0
-            and tile_rows == splits * SUBLANES
+            and members_axis == row_tiles * chunk_cols
+            and 2 * STEPS * CYCLES <= LANES // 2
         )
         if fits:
             return fast_body(members_axis, rows_axis, fields, bathymetry, copy_lists)

time: 38.1 us -> 35.5 us (0.932)
  the two profiles are of different devices: /device:TPU:0 before, /device:TPU:1 now
where the time goes in v7:
time: 35.5 us; the launch traced here: 35.3 us
  Pallas kernels  33.5 us (94%)
  local copies, waits for them, and re-layouts  1.77 us (5%)
    pallas_call x1, Pallas kernels, fast_body(): pl.pallas_call(functools.partial(kernel, members_axis, rows_axis), out_sh...  33.5 us
    unnamed x1, local copies, waits for them, and re-layouts  1.77 us

profile of v7, /device:TPU:1, one launch (start us, length us, event | category | flops | bytes accessed | tf_op | source)
XLA Modules:
  0.0 35.3 jit_solution(2488759352850953118)
XLA Ops:
  0.0 33.5 %shard_map.37 = f32[2,3,16,1024]{3,2,1,0:T(8,128)} custom-call(f32[2,3,16,1024]{3,2,1,0:T(8,128)} %fields.1, s32[16,1024]{1,0:T(8,128)} %bathymetry.1, s32[5,3,32]{2,1,0:T(4,128)} %bitcast.1), custom_call_target="tpu_custom_call" | custom-call | tf_op jit(solution)/shard_map/pallas_call | solution.py:367
  33.6 1.8 %copy.5 = f32[2,3,16,1024]{3,2,1,0:T(8,128)} copy(f32[2,3,16,1024]{3,2,1,0:T(8,128)} %shard_map.37) | data formatting | bytes 786432

commit v8 on v7

--- a/solution.py
+++ b/solution.py
@@ -249,15 +249,12 @@
                 for kind in range(3):
                     sent[q][kind, col, pl.ds(k, SUBLANES, stride=count)] = work[kind, k, :, here]
 
-    stages = [(q, kind) for q in range(CHUNKS) for kind in range(3)]
-
     def core_of(i):
-        return sum(stages[i]) % rows_axis
+        return i % rows_axis
 
     def spread_copy(i, j):
-        q, kind = stages[i]
-        src = sent[q].at[
-            kind,
+        src = sent[i].at[
+            :,
             lax.rem(j, chunk_cols),
             pl.ds(pl.multiple_of(j // chunk_cols * SUBLANES, SUBLANES), SUBLANES),
         ]
@@ -306,13 +303,12 @@
     home = my_row // tile_rows
 
     def place(i):
-        q, kind = stages[i]
         return out.at[
             :,
-            kind,
+            :,
             pl.ds(pl.multiple_of(lax.rem(my_row, tile_rows), SUBLANES), SUBLANES),
             pl.ds(
-                pl.multiple_of((q * chunk_cols + lax.rem(group, chunk_cols)) * LANES, LANES),
+                pl.multiple_of((i * chunk_cols + lax.rem(group, chunk_cols)) * LANES, LANES),
                 LANES,
             ),
         ]
@@ -327,13 +323,12 @@
 
     for q in range(CHUNKS):
         forecast(q)
-        for i in range(3 * q, 3 * q + 3):
-            send_all(
-                functools.partial(spread_copy, i),
-                row_no == core_of(i), held[i].at[me], spread_recv.at[i],
-            )
-
-    for i in range(len(stages)):
+        send_all(
+            functools.partial(spread_copy, q),
+            row_no == core_of(q), held[q].at[me], spread_recv.at[q],
+        )
+
+    for i in range(CHUNKS):
 
         @pl.when(row_no == core_of(i))
         def _(i=i):
@@ -344,15 +339,15 @@
                 functools.partial(back_copy, i), row_no == home, place(i), back_recv.at[i]
             )
 
-    for i, (q, kind) in enumerate(stages):
+    for i in range(CHUNKS):
         end_all(functools.partial(spread_copy, i), row_no == core_of(i))
 
         @pl.when(row_no == core_of(i))
         def _(i=i):
             end_all(functools.partial(back_copy, i), row_no == home)
 
-    for i, (q, kind) in enumerate(stages):
-        landed = out.at[:, kind, :, pl.ds(q * chunk_cols * LANES, chunk_cols * LANES)]
+    for i in range(CHUNKS):
+        landed = out.at[:, :, :, pl.ds(i * chunk_cols * LANES, chunk_cols * LANES)]
         pltpu.make_async_copy(landed, landed, back_recv.at[i]).wait()
 
 
@@ -385,17 +380,17 @@
             pltpu.VMEM((rows, width), jnp.int32),
             pltpu.VMEM((count, SUBLANES, chunk_width), f32),
             [pltpu.VMEM((kinds, width // LANES // CHUNKS, rows, LANES), f32)] * CHUNKS,
-            [pltpu.VMEM((members, SUBLANES, LANES), f32)] * (CHUNKS * kinds),
-            [pltpu.VMEM((members, SUBLANES, LANES), f32)] * (CHUNKS * kinds),
+            [pltpu.VMEM((members, kinds, SUBLANES, LANES), f32)] * CHUNKS,
+            [pltpu.VMEM((members, kinds, SUBLANES, LANES), f32)] * CHUNKS,
             pltpu.SMEM((copy_lists.shape[1], copy_lists.shape[0], copy_lists.shape[2]), jnp.int32),
             pltpu.SMEM((members,), jnp.int32),
             dma((3,)),
             dma((2 * rows_axis,)),
             dma((2 * rows_axis,)),
-            dma((CHUNKS * kinds, members_axis)),
-            dma((CHUNKS * kinds,)),
-            dma((CHUNKS * kinds, members_axis)),
-            dma((CHUNKS * kinds,)),
+            dma((CHUNKS, members_axis)),
+            dma((CHUNKS,)),
+            dma((CHUNKS, members_axis)),
+            dma((CHUNKS,)),
         ],
         compiler_params=pltpu.CompilerParams(
             collective_id=0, has_side_effects=True

time: 35.5 us -> 34.1 us (0.961)
  Pallas kernels: 33.5 us -> 32.2 us
    pallas_call x1, Pallas kernels: 33.5 us -> 32.2 us  [fast_body(): pl.pallas_call(functools.partial(kernel, members_axis, rows_axis), out_sh...]
where the time goes in v8:
time: 34.1 us; the launch traced here: 34 us
  Pallas kernels  32.2 us (94%)
  local copies, waits for them, and re-layouts  1.77 us (5%)
    pallas_call x1, Pallas kernels, fast_body(): pl.pallas_call(functools.partial(kernel, members_axis, rows_axis), out_sh...  32.2 us
    unnamed x1, local copies, waits for them, and re-layouts  1.77 us

profile of v8, /device:TPU:1, one launch (start us, length us, event | category | flops | bytes accessed | tf_op | source)
XLA Modules:
  0.0 34.0 jit_solution(14435005038939547417)
XLA Ops:
  0.0 32.2 %shard_map.37 = f32[2,3,16,1024]{3,2,1,0:T(8,128)} custom-call(f32[2,3,16,1024]{3,2,1,0:T(8,128)} %fields.1, s32[16,1024]{1,0:T(8,128)} %bathymetry.1, s32[5,3,32]{2,1,0:T(4,128)} %bitcast.1), custom_call_target="tpu_custom_call" | custom-call | tf_op jit(solution)/shard_map/pallas_call | solution.py:362
  32.2 1.8 %copy.5 = f32[2,3,16,1024]{3,2,1,0:T(8,128)} copy(f32[2,3,16,1024]{3,2,1,0:T(8,128)} %shard_map.37) | data formatting | bytes 786432

commit v9 on v8

--- a/solution.py
+++ b/solution.py
@@ -255,8 +255,8 @@
     def spread_copy(i, j):
         src = sent[i].at[
             :,
-            lax.rem(j, chunk_cols),
-            pl.ds(pl.multiple_of(j // chunk_cols * SUBLANES, SUBLANES), SUBLANES),
+            j // count,
+            pl.ds(pl.multiple_of(lax.rem(j, count) * SUBLANES, SUBLANES), SUBLANES),
         ]
         return src, pltpu.make_async_remote_copy(
             src_ref=src, dst_ref=held[i].at[me],
@@ -299,7 +299,7 @@
         def _():
             copy(group)[1].wait_send()
 
-    my_row = group // chunk_cols * SUBLANES
+    my_row = lax.rem(group, count) * SUBLANES
     home = my_row // tile_rows
 
     def place(i):
@@ -308,7 +308,7 @@
             :,
             pl.ds(pl.multiple_of(lax.rem(my_row, tile_rows), SUBLANES), SUBLANES),
             pl.ds(
-                pl.multiple_of((i * chunk_cols + lax.rem(group, chunk_cols)) * LANES, LANES),
+                pl.multiple_of((i * chunk_cols + group // count) * LANES, LANES),
                 LANES,
             ),
         ]
@@ -367,7 +367,7 @@
             pl.BlockSpec(memory_space=pltpu.HBM),
             pl.BlockSpec(memory_space=pltpu.HBM),
         ],
-        out_specs=pl.BlockSpec(memory_space=pltpu.VMEM),
+        out_specs=pl.BlockSpec(memory_space=pltpu.HBM),
         scratch_shapes=[
             pltpu.VMEM((kinds, rows, width), f32),
             pltpu.VMEM((kinds + 1, width // LANES, rows, LANES), f32),

time: 34.1 us -> 33.9 us (level)
  the two profiles are of different devices: /device:TPU:1 before, /device:TPU:0 now
where the time goes in v9:
time: 33.9 us; the launch traced here: 33.8 us
  Pallas kernels  32 us (94%)
  local copies, waits for them, and re-layouts  1.77 us (5%)
    pallas_call x1, Pallas kernels, fast_body(): pl.pallas_call(functools.partial(kernel, members_axis, rows_axis), out_sh...  32 us
    unnamed x1, local copies, waits for them, and re-layouts  1.77 us

profile of v9, /device:TPU:0, one launch (start us, length us, event | category | flops | bytes accessed | tf_op | source)
XLA Modules:
  0.0 33.8 jit_solution(10213599679628426940)
XLA Ops:
  0.0 32.0 %shard_map.37 = f32[2,3,16,1024]{3,2,1,0:T(8,128)} custom-call(f32[2,3,16,1024]{3,2,1,0:T(8,128)} %fields.1, s32[16,1024]{1,0:T(8,128)} %bathymetry.1, s32[5,3,32]{2,1,0:T(4,128)} %bitcast.1), custom_call_target="tpu_custom_call" | custom-call | tf_op jit(solution)/shard_map/pallas_call | solution.py:362
  32.0 1.8 %copy.5 = f32[2,3,16,1024]{3,2,1,0:T(8,128)} copy(f32[2,3,16,1024]{3,2,1,0:T(8,128)} %shard_map.37) | data formatting | bytes 786432
